TPU v7x, 256 devices: a whole 4x4x8 slice. The times are simulated.
256 devices in a mesh: comp: 2 (over core), blk: 32 (over z, x), sub: 4 (over y).
Axes of the slice: x: 4, y: 4, z: 8, core: 2. Of those that a mesh axis runs over, the one named last changes fastest.
Arguments:
- state: float32 [2, 4, 80, 262144], P('comp', None, None, ('blk', 'sub')), may hold values from -6 to 6
- tile_ops: float32 [2, 2048, 128, 128], P('comp', ('blk', 'sub')), may hold values from -0.5 to 0.5
- kappa: float32 [2, 80, 262144], P('comp', None, ('blk', 'sub')), may hold values from 0.1 to 8
- active: int32 [2, 2048], P('comp', ('blk', 'sub')), may hold values from 2 to 80
- edge_local: int32 [2, 131072], P('comp', ('blk', 'sub')), may hold values from 0 to 2047
- edge_halo: int32 [2, 131072], P('comp', ('blk', 'sub')), may hold values from 0 to 1023
- edge_coef: float32 [2, 131072], P('comp', ('blk', 'sub')), may hold values from 0.25 to 2
- remap_src: int32 [2, 16384], P('comp', ('blk', 'sub')), may hold values from 0 to 15
- remap_owner: int32 [2, 16384, 1], P('comp', ('blk', 'sub')), may hold values from 0 to 127; in each aligned block of 128 rows (0 to 127, 128 to 255, ..., all dimensions but the last counted through in order) at most 2 rows name the same one
- remap_tile: int32 [2, 16384], P('comp', ('blk', 'sub')), may hold values from 0 to 15
- remap_weight: bfloat16 [2, 16384, 128, 128], P('comp', ('blk', 'sub')), may hold values from -0.1875 to 0.1875
Outputs:
- new_state: float32 [2, 4, 80, 262144], P('comp', None, None, ('blk', 'sub'))
- coupled_flux: float32 [2, 4, 262144], P('comp', None, ('blk', 'sub'))
Inputs may be any that keep to these rules, and one draw needn't show every extreme that they name: `remap_owner`: within the 128 remap tiles of one device no owner is named more than 2 times, a bound that some block reaches.
All inputs are finite; a program needn't handle non-finite values.
Results may differ from a plain program's by a relative error of at most 0.0029.
Values sent between devices are 32-bit elements; how exact they have to be, the bound alone decides.
No kernel may reach another device: no remote copies, remote signals or barrier semaphores. Data moves between devices by JAX's collectives and lax.ppermute only.
A program may use at most 128 MiB of HBM per device.

v0:
```python
import jax
import jax.numpy as jnp
from jax import lax
from jax.experimental import pallas as pl
from jax.experimental.pallas import tpu as pltpu
from jax.sharding import PartitionSpec as P

HALO_W = 512
LANES = 128
STEP = 0.25
RELAX = 0.5
CHUNK = 9
F32 = jnp.float32
BF16 = jnp.bfloat16
VMEM = pltpu.VMEM
SMEM = pltpu.SMEM


def split3(x):
    hi = x.astype(BF16)
    rest = x - hi.astype(F32)
    mid = rest.astype(BF16)
    low = (rest - mid.astype(F32)).astype(BF16)
    return hi, mid, low


def split2(x):
    hi = x.astype(BF16)
    return hi, (x - hi.astype(F32)).astype(BF16)


def mm(a, b):
    return jnp.dot(a, b, preferred_element_type=F32)


def vspec():
    return pl.BlockSpec(memory_space=VMEM)


def sspec():
    return pl.BlockSpec(memory_space=SMEM)


def hbm(x):
    return pltpu.with_memory_space_constraint(x, pltpu.HBM)


def aspec():
    return pl.BlockSpec(memory_space=pltpu.HBM)


def params(mib):
    return pltpu.CompilerParams(vmem_limit_bytes=mib * 1024 * 1024)


def sides(even_ref, columns):
    even = even_ref[0] == 1
    last = columns - HALO_W
    return [pl.multiple_of(jnp.where(even, *pair), LANES) for pair in ((last, 0), (0, last))]


def pack_top_body(even_ref, state_ref, one_ref, two_ref, window, sem):
    loads = [
        pltpu.make_async_copy(state_ref.at[0, :, pl.ds(0, 8), pl.ds(at, HALO_W)], window.at[i], sem.at[i])
        for i, at in enumerate(sides(even_ref, state_ref.shape[3]))
    ]
    for load in loads:
        load.start()
    for i, ref in enumerate((one_ref, two_ref)):
        loads[i].wait()
        ref[...] = window[i, :, 0, :]


def pack_top(even, state):
    fields = state.shape[1]
    return pl.pallas_call(
        pack_top_body,
        in_specs=[sspec(), aspec()],
        out_specs=[vspec()] * 2,
        out_shape=[jax.ShapeDtypeStruct((fields, HALO_W), F32)] * 2,
        scratch_shapes=[pltpu.VMEM((2, fields, 8, HALO_W), F32), pltpu.SemaphoreType.DMA((2,))],
        cost_estimate=pl.CostEstimate(flops=0, bytes_accessed=10**5, transcendentals=0),
    )(even, hbm(state))


def pack_body(even_ref, state_ref, _, one_ref, two_ref, sem):
    loads = [
        pltpu.make_async_copy(state_ref.at[0, :, :, pl.ds(at, HALO_W)], ref, sem.at[i])
        for i, (at, ref) in enumerate(zip(sides(even_ref, state_ref.shape[3]), (one_ref, two_ref)))
    ]
    for load in loads:
        load.start()
    for load in loads:
        load.wait()


def pack(even, state, after):
    _, fields, levels, _ = state.shape
    return pl.pallas_call(
        pack_body,
        in_specs=[sspec(), aspec(), pl.BlockSpec(memory_space=pl.ANY)],
        out_specs=[vspec()] * 2,
        out_shape=[jax.ShapeDtypeStruct((fields, levels, HALO_W), F32)] * 2,
        scratch_shapes=[pltpu.SemaphoreType.DMA((2,))],
        cost_estimate=pl.CostEstimate(flops=0, bytes_accessed=3 * 10**6, transcendentals=0),
    )(even, hbm(state), after)


def gather_halo(pick, index, coef):
    rows = pick(0).shape[0]
    lane = jnp.broadcast_to(jnp.bitwise_and(index, LANES - 1), (rows, LANES))
    part = jnp.broadcast_to(jnp.right_shift(index, 7), (rows, LANES))
    found = jnp.zeros((rows, LANES), F32)
    for h in range(2 * HALO_W // LANES):
        got = jnp.take_along_axis(pick(h), lane, axis=1)
        found = jnp.where(part == h, got, found)
    return found * coef


def rows_of(ref):
    return jnp.concatenate([ref[block : block + 1, :] for block in range(ref.shape[0])], axis=1)


def remap_body(
    one_ref, two_ref, state_ref, ops_ref, local_ref, halo_ref, coef_ref, src_ref, owner_ref, tile_ref, weight_ref,
    star_ref, total_ref, out_ref, window, ops, weights, first_s, second_s, pairs, products, sem,
):
    fields, columns = star_ref.shape
    tiles = columns // LANES
    remaps = weight_ref.shape[0]
    group = out_ref.shape[0] // CHUNK
    parts = 4
    size = remaps // parts
    copies = [
        pltpu.make_async_copy(weight_ref.at[pl.ds(i * size, size)], weights.at[pl.ds(i * size, size)], sem.at[i])
        for i in range(parts)
    ]
    load = pltpu.make_async_copy(state_ref.at[0, :, pl.ds(0, 8), :], window, sem.at[parts])
    load_ops = pltpu.make_async_copy(ops_ref, ops, sem.at[parts + 1])
    load.start()
    load_ops.start()
    for copy in copies:
        copy.start()

    per = HALO_W // LANES

    def pick(h):
        ref = one_ref if h < per else two_ref
        h = h % per
        return ref[:, h * LANES : (h + 1) * LANES]

    blocks = halo_ref.shape[0]
    flow = jnp.concatenate(
        [gather_halo(pick, halo_ref[k : k + 1, :], coef_ref[k : k + 1, :]) for k in range(blocks)], axis=1
    )
    coef = rows_of(coef_ref)
    own = rows_of(local_ref)
    own_tile = jnp.right_shift(own, 7)
    stack = jnp.concatenate([flow, coef], axis=0)
    wide = jnp.concatenate([jnp.where(own_tile == t, stack, 0.0) for t in range(tiles)], axis=0)
    across = jnp.transpose(jnp.bitwise_and(local_ref[...], LANES - 1))
    lane = lax.broadcasted_iota(jnp.int32, (LANES, LANES), 1)
    hot = jnp.concatenate(
        [
            jnp.where(jnp.broadcast_to(across[:, k : k + 1], (LANES, LANES)) == lane, 1.0, 0.0).astype(BF16)
            for k in range(blocks)
        ],
        axis=0,
    )
    spread = sum(mm(part, hot) for part in split3(wide))
    load.wait()
    load_ops.wait()
    for tile in range(tiles):
        where = slice(tile * LANES, (tile + 1) * LANES)
        here = window[:, 0, where]
        mixed = jnp.dot(here, ops[tile], precision=lax.Precision.HIGHEST, preferred_element_type=F32)
        base = tile * (fields + 1)
        total = spread[base + fields : base + fields + 1]
        total_ref[:, where] = jnp.broadcast_to(total, (total_ref.shape[0], LANES))
        star = here + STEP * (mixed + (spread[base : base + fields] - total * here))
        star_ref[:, where] = star
        surface = star.astype(BF16).astype(F32)
        nothing = jnp.zeros_like(surface)
        first_s[tile] = jnp.concatenate([surface, nothing], axis=0)
        second_s[tile] = jnp.concatenate([nothing, surface], axis=0)
    for pair in range(remaps // 2):
        left = first_s[src_ref[2 * pair]]
        right = second_s[src_ref[2 * pair + 1]]
        pairs[pair] = jnp.concatenate([left, right], axis=1)
    for part in range(parts):
        copies[part].wait()
        for pair in range(part * size // 2, (part + 1) * size // 2):
            weight = weights[2 * pair : 2 * pair + 2].reshape(2 * LANES, LANES)
            products[2 * fields * pair : 2 * fields * (pair + 1)] = mm(pairs[pair].astype(BF16), weight)

    owner = owner_ref[...]
    down = lax.broadcasted_iota(jnp.int32, (remaps, remaps), 0)
    right = lax.broadcasted_iota(jnp.int32, (remaps, remaps), 1)
    owner_rows = jnp.broadcast_to(owner, (remaps, remaps))
    owner_columns = jnp.transpose(owner_rows)
    earlier = jnp.where((owner_rows == owner_columns) & (down < right), 1, 0)
    rank = jnp.sum(earlier, axis=0, keepdims=True)
    dest = lax.broadcasted_iota(jnp.int32, (group, remaps), 0)
    named = jnp.broadcast_to(owner, (group, remaps)) == dest
    slots = [named & (jnp.broadcast_to(rank, (group, remaps)) == k) for k in range(2)]
    place = jnp.concatenate([jnp.where(slot, 1.0, 0.0).astype(BF16) for slot in slots], axis=0)
    wanted = tile_ref[...]
    labels = [jnp.max(jnp.where(slot, wanted, -1), axis=1, keepdims=True) for slot in slots]
    side = lax.broadcasted_iota(jnp.int32, (group, LANES), 1)
    note = jnp.where(side == 0, labels[0], jnp.where(side == 1, labels[1], -1))
    out_ref[pl.ds(2 * fields, group, stride=CHUNK), :] = note.astype(F32)
    for field in range(fields):
        value = products[pl.ds(field, remaps, stride=fields), :]
        placed = sum(mm(place, part) for part in split3(value))
        for k in range(2):
            out_ref[pl.ds(k * fields + field, group, stride=CHUNK), :] = placed[k * group : (k + 1) * group]


def remap(one, two, state, ops, edge_local, edge_halo, edge_coef, src, owners, wanted, weight, group):
    _, fields, _, columns = state.shape
    remaps = weight.shape[0]
    blocks = edge_halo.size // LANES
    tiles = columns // LANES
    fold = lambda x: x.reshape(blocks, LANES)
    return pl.pallas_call(
        remap_body,
        in_specs=[vspec()] * 2 + [aspec()] * 2 + [vspec()] * 3 + [sspec(), vspec(), vspec(), aspec()],
        out_specs=[vspec()] * 3,
        out_shape=[
            jax.ShapeDtypeStruct((fields, columns), F32),
            jax.ShapeDtypeStruct((8, columns), F32),
            jax.ShapeDtypeStruct((group * CHUNK, LANES), F32),
        ],
        scratch_shapes=[
            pltpu.VMEM((fields, 8, columns), F32),
            pltpu.VMEM(ops.shape, F32),
            pltpu.VMEM(weight.shape, BF16),
            pltpu.VMEM((tiles, 2 * fields, LANES), F32),
            pltpu.VMEM((tiles, 2 * fields, LANES), F32),
            pltpu.VMEM((remaps // 2, 2 * fields, 2 * LANES), F32),
            pltpu.VMEM((remaps * fields, LANES), F32),
            pltpu.SemaphoreType.DMA((6,)),
        ],
        compiler_params=params(16),
        cost_estimate=pl.CostEstimate(flops=6 * 10**10, bytes_accessed=6 * 10**6, transcendentals=0),
    )(
        one, two, hbm(state), hbm(ops), fold(edge_local), fold(edge_halo), fold(edge_coef), src,
        owners.reshape(1, remaps), wanted.reshape(1, remaps), hbm(weight),
    )


def column_body(
    one_ref, two_ref, local_ref, halo_ref, coef_ref, state_ref, ops_ref, total_ref, star_ref, kappa_ref,
    active_ref, base_ref, gain_ref, flow_hi, flow_lo, work, inv, up, down,
):
    step = pl.program_id(0)
    _, fields, levels, width = state_ref.shape
    rows = fields * levels
    per = HALO_W // LANES
    blocks = halo_ref.shape[0]
    tiles = range(width // LANES)
    cut = [slice(tile * LANES, (tile + 1) * LANES) for tile in tiles]

    @pl.when(step == 0)
    def _():
        def pick(h):
            where = slice((h % per) * LANES, (h % per + 1) * LANES)
            ref = one_ref if h < per else two_ref
            return ref[:, :, where].reshape(rows, LANES)

        for k in range(blocks):
            hi, lo = split2(gather_halo(pick, halo_ref[k : k + 1, :], coef_ref[k : k + 1, :]))
            flow_hi[:, k * LANES : (k + 1) * LANES] = hi
            flow_lo[:, k * LANES : (k + 1) * LANES] = lo

    across = jnp.transpose(local_ref[...] - step * width)
    lane = lax.broadcasted_iota(jnp.int32, (LANES, LANES), 1)
    hot = []
    for k in range(blocks):
        own = jnp.broadcast_to(across[:, k : k + 1], (LANES, LANES)) - lane
        hot.append(jnp.concatenate([jnp.where(own == t * LANES, 1.0, 0.0).astype(BF16) for t in tiles], axis=1))
    hot = jnp.concatenate(hot, axis=0)
    extra = mm(flow_hi[...], hot) + mm(flow_lo[...], hot)
    for tile in tiles:
        here = state_ref[0, :, :, cut[tile]].reshape(rows, LANES)
        a_hi, a_lo = split2(here)
        b_hi, b_lo = split2(ops_ref[tile])
        mixed = mm(a_hi, b_hi) + (mm(a_hi, b_lo) + mm(a_lo, b_hi))
        work[tile] = here + STEP * ((mixed - here * total_ref[0:1, cut[tile]]) + extra[:, cut[tile]])

    depth = lax.broadcasted_iota(jnp.int32, (levels, LANES), 0)
    for tile in tiles:
        count = active_ref[step * len(tiles) + tile]
        down[:, cut[tile]] = jnp.where(depth + 1 < count, -STEP * kappa_ref[0, :, cut[tile]], 0.0)
    last = levels - 1
    upper = down[last : last + 1, :]
    lower = down[last - 1 : last, :]
    inverse = 1.0 / (1.0 - lower - upper)
    ratio = lower * inverse
    inv[last : last + 1, :] = inverse
    up[last : last + 1, :] = upper * inverse
    down[last : last + 1, :] = ratio
    for level in range(last - 1, -1, -1):
        row = slice(level, level + 1)
        upper = lower
        lower = down[level - 1 : level, :] if level else jnp.zeros_like(upper)
        inverse = 1.0 / (1.0 - lower - upper - upper * ratio)
        ratio = lower * inverse
        inv[row, :] = inverse
        up[row, :] = upper * inverse
        down[row, :] = ratio
    gain = RELAX * inverse
    gain_ref[0:1, :] = gain
    for level in range(1, levels):
        gain = -gain * down[level : level + 1, :]
        gain_ref[level : level + 1, :] = gain

    values = [None for _ in tiles]
    for level in range(last, -1, -1):
        row = slice(level, level + 1)
        spot = pl.ds(level, fields, stride=levels)
        for tile in tiles:
            rhs = work[tile, spot, :] if level else RELAX * star_ref[:, cut[tile]]
            scaled = rhs * inv[row, cut[tile]]
            value = values[tile]
            values[tile] = scaled if value is None else scaled - up[row, cut[tile]] * value
            work[tile, spot, :] = values[tile]
    for level in range(1, levels):
        row = slice(level, level + 1)
        spot = pl.ds(level, fields, stride=levels)
        for tile in tiles:
            values[tile] = work[tile, spot, :] - down[row, cut[tile]] * values[tile]
            work[tile, spot, :] = values[tile]
    for tile in tiles:
        base_ref[:, :, cut[tile]] = work[tile].reshape(fields, levels, LANES)


def column_part(one, two, edge_local, edge_halo, edge_coef, state, ops, total, star, kappa, active):
    _, fields, levels, columns = state.shape
    steps = 4
    width = columns // steps
    edges = edge_halo.size
    blocks = edges // LANES
    column = pl.BlockSpec((levels, width), lambda i: (0, i))
    whole = lambda x: pl.BlockSpec(x.shape, lambda i: (0,) * x.ndim)
    lists = [x.reshape(blocks, LANES) for x in (edge_local, edge_halo, edge_coef)]
    return pl.pallas_call(
        column_body,
        grid=(steps,),
        in_specs=[whole(x) for x in (one, two, *lists)]
        + [
            pl.BlockSpec((1, fields, levels, width), lambda i: (0, 0, 0, i)),
            pl.BlockSpec((width // LANES, LANES, LANES), lambda i: (i, 0, 0)),
            pl.BlockSpec((8, width), lambda i: (0, i)),
            pl.BlockSpec((fields, width), lambda i: (0, i)),
            pl.BlockSpec((1, levels, width), lambda i: (0, 0, i)),
            sspec(),
        ],
        out_specs=[pl.BlockSpec((fields, levels, width), lambda i: (0, 0, i)), column],
        out_shape=[
            jax.ShapeDtypeStruct((fields, levels, columns), F32),
            jax.ShapeDtypeStruct((levels, columns), F32),
        ],
        scratch_shapes=[
            pltpu.VMEM((fields * levels, edges), BF16),
            pltpu.VMEM((fields * levels, edges), BF16),
            pltpu.VMEM((width // LANES, fields * levels, LANES), F32),
            pltpu.VMEM((levels, width), F32),
            pltpu.VMEM((levels, width), F32),
            pltpu.VMEM((levels, width), F32),
        ],
        compiler_params=params(24),
        cost_estimate=pl.CostEstimate(flops=6 * 10**10, bytes_accessed=10**7, transcendentals=0),
    )(one, two, *lists, hbm(state), hbm(ops), total, star, hbm(kappa), active)


def gather_body(arrived_ref, _, flux_ref):
    fields, tiles, _ = flux_ref.shape
    sources = arrived_ref.shape[0] // CHUNK
    labels = jnp.transpose(arrived_ref[pl.ds(2 * fields, sources, stride=CHUNK), :])
    tile = lax.broadcasted_iota(jnp.int32, (tiles, sources), 0).astype(F32)
    select = jnp.concatenate(
        [jnp.where(tile == labels[k : k + 1, :], 1.0, 0.0).astype(BF16) for k in range(2)], axis=1
    )
    for field in range(fields):
        value = jnp.concatenate(
            [arrived_ref[pl.ds(k * fields + field, sources, stride=CHUNK), :] for k in range(2)], axis=0
        )
        flux_ref[field] = sum(mm(select, part) for part in split3(value))


def gather_flux(arrived, after, fields, tiles):
    return pl.pallas_call(
        gather_body,
        in_specs=[vspec(), pl.BlockSpec(memory_space=pl.ANY)],
        out_specs=vspec(),
        out_shape=jax.ShapeDtypeStruct((fields, tiles, LANES), F32),
        cost_estimate=pl.CostEstimate(flops=10**6, bytes_accessed=10**6, transcendentals=0),
    )(arrived, after)


def finish_body(base_ref, gain_ref, flux_ref, active_ref, out_ref, flux_out):
    step = pl.program_id(0)
    fields, levels, width = base_ref.shape
    depth = lax.broadcasted_iota(jnp.int32, (levels, LANES), 0)
    for tile in range(width // LANES):
        where = slice(tile * LANES, (tile + 1) * LANES)
        place = step * (width // LANES) + tile
        inside = depth < active_ref[place]
        gain = gain_ref[:, where]
        for field in range(fields):
            flux = flux_ref[field, pl.ds(place, 1), :]
            flux_out[0, field : field + 1, where] = flux
            out_ref[0, field, :, where] = jnp.where(inside, base_ref[field, :, where] + gain * flux, 0.0)


def finish(base, gain, flux, active):
    fields, levels, columns = base.shape
    steps = 4
    width = columns // steps
    return pl.pallas_call(
        finish_body,
        grid=(steps,),
        in_specs=[
            pl.BlockSpec((fields, levels, width), lambda i: (0, 0, i)),
            pl.BlockSpec((levels, width), lambda i: (0, i)),
            pl.BlockSpec(flux.shape, lambda i: (0, 0, 0)),
            sspec(),
        ],
        out_specs=[
            pl.BlockSpec((1, fields, levels, width), lambda i: (0, 0, 0, i)),
            pl.BlockSpec((1, fields, width), lambda i: (0, 0, i)),
        ],
        out_shape=[
            jax.ShapeDtypeStruct((1, fields, levels, columns), F32),
            jax.ShapeDtypeStruct((1, fields, columns), F32),
        ],
        compiler_params=params(24),
        cost_estimate=pl.CostEstimate(flops=10**7, bytes_accessed=6 * 10**6, transcendentals=0),
    )(base, gain, flux, active)


def local(
    state, tile_ops, kappa, active, edge_local, edge_halo, edge_coef, remap_src, remap_owner, remap_tile, remap_weight
):
    _, fields, levels, columns = state.shape
    tiles = tile_ops.shape[1]
    remaps = remap_src.shape[1]
    axes = ("blk", "sub")
    group = lax.axis_size("blk") * lax.axis_size("sub")
    first = [(i, i ^ 1) for i in range(group)]
    second = [(i, (i + 1) % group if i % 2 else (i - 1) % group) for i in range(group)]
    even = (1 - lax.axis_index("sub") % 2).astype(jnp.int32).reshape(1)
    count = active.reshape(tiles)
    halo = jnp.bitwise_xor(edge_halo, HALO_W * even[0])

    top_one, top_two = pack_top(even, state)
    one, two = pack(even, state, top_one)
    top_one = lax.ppermute(top_one, axes, first)
    top_two = lax.ppermute(top_two, axes, second)
    one = lax.ppermute(one, axes, first)
    two = lax.ppermute(two, axes, second)
    star0, total, outgoing = remap(
        top_one, top_two, state, tile_ops[0], edge_local, halo, edge_coef, remap_src.reshape(remaps),
        remap_owner, remap_tile, remap_weight[0], group,
    )
    arrived = lax.all_to_all(
        outgoing.reshape(group, 1, CHUNK * LANES), axes, split_axis=0, concat_axis=0, tiled=True
    )
    base, gain = column_part(
        one, two, edge_local, halo, edge_coef, state, tile_ops[0], total, star0, kappa, count
    )
    flux = gather_flux(arrived.reshape(group * CHUNK, LANES), gain, fields, tiles)
    flux = lax.ppermute(flux, "comp", [(0, 1), (1, 0)])
    return finish(base, gain, flux, count)


def solution(mesh):
    placed = (
        P("comp", None, None, ("blk", "sub")),
        P("comp", ("blk", "sub"), None, None),
        P("comp", None, ("blk", "sub")),
        P("comp", ("blk", "sub")),
        P("comp", ("blk", "sub")),
        P("comp", ("blk", "sub")),
        P("comp", ("blk", "sub")),
        P("comp", ("blk", "sub")),
        P("comp", ("blk", "sub"), None),
        P("comp", ("blk", "sub")),
        P("comp", ("blk", "sub"), None, None),
    )
    return jax.shard_map(
        local,
        mesh=mesh,
        in_specs=placed,
        out_specs=(P("comp", None, None, ("blk", "sub")), P("comp", None, ("blk", "sub"))),
        check_vma=False,
    )
```

profile of v0, /device:TPU:1, one launch (start us, length us, event | category | flops | bytes accessed | tf_op | source)
XLA Modules:
  0.0 64.3 jit_solution(2726187602953289843)
XLA Ops:
  0.6 0.0 copy-start.10
  0.7 0.0 copy-start.5
  0.7 0.0 copy-start.6
  0.7 0.0 copy-start.7
  0.7 0.0 copy-start.8
  0.7 0.0 copy-start.9
  0.7 1.5 %shard_map.122 = (f32[4,512]{1,0:T(4,128)}, f32[4,512]{1,0:T(4,128)}) custom-call(s32[1]{0:T(128)} %bitcast.even_ref, f32[1,4,80,2048]{3,2,1,0:T(8,128)} %state_ref.7), custom_call_target="tpu_custom_call" | custom-call | bytes 100000 | tf_op jit(solution)/shard_map/pallas_call | solution.py:76
  2.2 11.1 %collective-permute-start.3 = (f32[4,512]{1,0:T(4,128)}, f32[4,512]{1,0:T(4,128)S(1)}, u32[]{:S(2)}, u32[]{:S(2)}) collective-permute-start(f32[4,512]{1,0:T(4,128)} %get-tuple-element.14), channel_id=1, source_target_pairs={{0,127},{1,2},{2,1},{3,4},{4,3},{5,6},{6,5},{7,8},{8,7},{9,10},{10... | collective-permute-start | bytes 24584 | tf_op jit(solution)/shard_map/ppermute | solution.py:460
  13.4 0.0 collective-permute-start.2
  13.4 2.4 %shard_map.123 = (f32[4,80,512]{2,1,0:T(8,128)}, f32[4,80,512]{2,1,0:T(8,128)}) custom-call(s32[1]{0:T(128)} %bitcast.even_ref, f32[1,4,80,2048]{3,2,1,0:T(8,128)} %state_ref.7, f32[4,512]{1,0:T(4,128)} %get-tuple-element.11._), custom_call_target="tpu_custom_call" | custom-call | bytes 3000000 | tf_op jit(solution)/shard_map/pallas_call | solution.py:99
  15.8 1.5 %collective-permute-start = (f32[4,80,512]{2,1,0:T(8,128)}, f32[4,80,512]{2,1,0:T(8,128)S(1)}, u32[]{:S(2)}, u32[]{:S(2)}) collective-permute-start(f32[4,80,512]{2,1,0:T(8,128)} %get-tuple-element.12), channel_id=1, source_target_pairs={{0,1},{1,0},{2,3},{3,2},{4,5},{5,4},{6,7},{7,6},{8,9},{9,8},{10,11... | collective-permute-start | bytes 1966088 | tf_op jit(solution)/shard_map/ppermute | solution.py:461
  17.3 0.1 collective-permute-start.1
  17.4 0.0 collective-permute-done.3.two_ref
  17.4 0.0 collective-permute-done.2.one_ref
  17.4 0.0 copy-done.5
  17.5 0.0 copy-done.6
  17.5 0.0 copy-start.2
  17.5 5.5 %shard_map.124 = (f32[4,2048]{1,0:T(4,128)S(1)}, f32[8,2048]{1,0:T(8,128)S(1)}, f32[1152,128]{1,0:T(8,128)}) custom-call(f32[4,512]{1,0:T(4,128)S(1)} %collective-permute-done.2.one_ref, f32[4,512]{1,0:T(4,128)S(1)} %collective-permute-done.3.two_ref, f32[1,4,80,2048]{3,2,1,0:T(8,128)} %state_ref.7, f32[16,128,128]{2,1,0:T(8,128)} %bitcast.22, ...), custom_call_target="tpu_custom_call" | custom-call | flops 60000002048 | bytes 6000000 | tf_op jit(solution)/shard_map/pallas_call | solution.py:225
  23.0 10.9 %all-to-all-start = ((f32[128,1,1152]{2,1,0:T(1,128)}), f32[128,1,1152]{2,1,0:T(1,128)}, u32[]{:S(2)}, u32[]{:S(2)}) async-start(f32[128,1,1152]{2,1,0:T(1,128)} %bitcast.9), calls=%async_computation | async-start | bytes 1179648 | tf_op jit(solution)/shard_map/all_to_all | solution.py:467
  34.0 0.0 collective-permute-done.one_ref
  34.0 3.7 %collective-permute-done.1.two_ref = f32[4,80,512]{2,1,0:T(8,128)S(1)} collective-permute-done((f32[4,80,512]{2,1,0:T(8,128)}, f32[4,80,512]{2,1,0:T(8,128)S(1)}, u32[]{:S(2)}, u32[]{:S(2)}) %collective-permute-start.1) | collective-permute-done | bytes 655392 | tf_op jit(solution)/shard_map/ppermute | solution.py:462
  37.7 0.8 %copy-done.3 = f32[4,80,512]{2,1,0:T(8,128)} copy-done((f32[4,80,512]{2,1,0:T(8,128)}, f32[4,80,512]{2,1,0:T(8,128)S(1)}, u32[]{:S(2)}) %copy-start.3) | copy-done | bytes 655384
  38.5 1.1 %copy-done.4 = f32[4,80,512]{2,1,0:T(8,128)S(1)} copy-done((f32[4,80,512]{2,1,0:T(8,128)S(1)}, f32[4,80,512]{2,1,0:T(8,128)}, u32[]{:S(2)}) %copy-start.4) | copy-done | bytes 655384
  39.6 13.7 %shard_map.125 = (f32[4,80,2048]{2,1,0:T(8,128)S(1)}, f32[80,2048]{1,0:T(8,128)S(1)}) custom-call(f32[4,80,512]{2,1,0:T(8,128)S(1)} %collective-permute-done.one_ref, f32[4,80,512]{2,1,0:T(8,128)S(1)} %copy-done.4, s32[8,128]{1,0:T(8,128)S(1)} %bitcast.16, s32[8,128]{1,0:T(8,128)S(1)} %bitcast.12, f32[8,128]{1,0:T(8,128)S(1)} %bitcast.18, ...), custom_call_target="tpu_custom_call" | custom-call | flops 60000002048 | bytes 10000000 | tf_op jit(solution)/shard_map/pallas_call | solution.py:347
  53.3 0.0 copy-start
  53.3 0.8 %copy-done = f32[80,2048]{1,0:T(8,128)} copy-done((f32[80,2048]{1,0:T(8,128)}, f32[80,2048]{1,0:T(8,128)S(1)}, u32[]{:S(2)}) %copy-start) | copy-done | bytes 655384
  54.2 0.0 all-to-all-done
  54.2 2.0 %shard_map.126 = f32[4,16,128]{2,1,0:T(8,128)} custom-call(f32[1152,128]{1,0:T(8,128)} %bitcast.10.arrived_ref, f32[80,2048]{1,0:T(8,128)} %copy-done), custom_call_target="tpu_custom_call" | custom-call | flops 1000000 | bytes 1000000 | tf_op jit(solution)/shard_map/pallas_call | solution.py:393
  56.1 3.3 %collective-permute-start.4 = (f32[4,16,128]{2,1,0:T(8,128)}, f32[4,16,128]{2,1,0:T(8,128)S(1)}, u32[]{:S(2)}, u32[]{:S(2)}) collective-permute-start(f32[4,16,128]{2,1,0:T(8,128)} %shard_map.126), channel_id=1, source_target_pairs={{0,128},{128,0},{1,129},{129,1},{2,130},{130,2},{3,131},{131,3},{4... | collective-permute-start | bytes 98312 | tf_op jit(solution)/shard_map/ppermute | solution.py:474
  59.4 1.1 %collective-permute-done.4.flux_ref = f32[4,16,128]{2,1,0:T(8,128)S(1)} collective-permute-done((f32[4,16,128]{2,1,0:T(8,128)}, f32[4,16,128]{2,1,0:T(8,128)S(1)}, u32[]{:S(2)}, u32[]{:S(2)}) %collective-permute-start.4) | collective-permute-done | bytes 32800 | tf_op jit(solution)/shard_map/ppermute | solution.py:474
  60.5 1.1 %copy-done.1 = f32[80,2048]{1,0:T(8,128)S(1)} copy-done((f32[80,2048]{1,0:T(8,128)S(1)}, f32[80,2048]{1,0:T(8,128)}, u32[]{:S(2)}) %copy-start.1) | copy-done | bytes 655384
  61.5 2.8 %shard_map.127 = (f32[1,4,80,2048]{3,2,1,0:T(8,128)}, f32[1,4,2048]{2,1,0:T(4,128)}) custom-call(f32[4,80,2048]{2,1,0:T(8,128)S(1)} %get-tuple-element.17.base_ref, f32[80,2048]{1,0:T(8,128)S(1)} %copy-done.1, f32[4,16,128]{2,1,0:T(8,128)S(1)} %collective-permute-done.4.flux_ref, s32[16]{0:T(128)S(1)} %bitcast.14), custom_call_target="tpu_custom_call" | custom-call | flops 10000000 | bytes 6000000 | tf_op jit(solution)/shard_map/pallas_call | solution.py:421
  (9 shorter events, 0.0 us)
Async XLA Ops:
  0.6 16.8 %copy-start.10 = (s32[1,1024]{1,0:T(1,128)S(1)}, s32[1,1024]{1,0:T(1,128)}, u32[]{:S(2)}) copy-start(s32[1,1024]{1,0:T(1,128)} %param.16) | copy-start | bytes 12292
  0.7 16.8 %copy-start.5 = (s32[1,1024]{1,0:T(1,128)S(1)}, s32[1,1024]{1,0:T(1,128)}, u32[]{:S(2)}) copy-start(s32[1,1024]{1,0:T(1,128)} %param.15) | copy-start | bytes 12292
  0.7 16.8 %copy-start.6 = (f32[1,1024]{1,0:T(1,128)S(1)}, f32[1,1024]{1,0:T(1,128)}, u32[]{:S(2)}) copy-start(f32[1,1024]{1,0:T(1,128)} %param.17) | copy-start | bytes 12292
  0.7 16.8 %copy-start.7 = (s32[1,128]{1,0:T(1,128)S(1)}, s32[1,128]{1,0:T(1,128)}, u32[]{:S(2)}) copy-start(s32[1,128]{1,0:T(1,128)} %param.18) | copy-start | bytes 1540
  0.7 16.8 %copy-start.8 = (s32[1,128,1]{1,2,0:T(1,128)S(1)}, s32[1,128,1]{1,2,0:T(1,128)}, u32[]{:S(2)}) copy-start(s32[1,128,1]{1,2,0:T(1,128)} %param.19) | copy-start | bytes 1540
  0.7 16.8 %copy-start.9 = (s32[1,128]{1,0:T(1,128)S(1)}, s32[1,128]{1,0:T(1,128)}, u32[]{:S(2)}) copy-start(s32[1,128]{1,0:T(1,128)} %tile_ref.1) | copy-start | bytes 1540
  2.2 15.2 %collective-permute-start.3 = (f32[4,512]{1,0:T(4,128)}, f32[4,512]{1,0:T(4,128)S(1)}, u32[]{:S(2)}, u32[]{:S(2)}) collective-permute-start(f32[4,512]{1,0:T(4,128)} %get-tuple-element.14), channel_id=1, source_target_pairs={{0,127},{1,2},{2,1},{3,4},{4,3},{5,6},{6,5},{7,8},{8,7},{9,10},{10... | collective-permute-start | bytes 24584 | tf_op jit(solution)/shard_map/ppermute | solution.py:460
  13.4 4.1 %collective-permute-start.2 = (f32[4,512]{1,0:T(4,128)}, f32[4,512]{1,0:T(4,128)S(1)}, u32[]{:S(2)}, u32[]{:S(2)}) collective-permute-start(f32[4,512]{1,0:T(4,128)} %get-tuple-element.11._), channel_id=1, source_target_pairs={{0,1},{1,0},{2,3},{3,2},{4,5},{5,4},{6,7},{7,6},{8,9},{9,8},{10,11... | collective-permute-start | bytes 24584 | tf_op jit(solution)/shard_map/ppermute | solution.py:459
  15.8 18.2 %collective-permute-start = (f32[4,80,512]{2,1,0:T(8,128)}, f32[4,80,512]{2,1,0:T(8,128)S(1)}, u32[]{:S(2)}, u32[]{:S(2)}) collective-permute-start(f32[4,80,512]{2,1,0:T(8,128)} %get-tuple-element.12), channel_id=1, source_target_pairs={{0,1},{1,0},{2,3},{3,2},{4,5},{5,4},{6,7},{7,6},{8,9},{9,8},{10,11... | collective-permute-start | bytes 1966088 | tf_op jit(solution)/shard_map/ppermute | solution.py:461
  17.3 20.3 %collective-permute-start.1 = (f32[4,80,512]{2,1,0:T(8,128)}, f32[4,80,512]{2,1,0:T(8,128)S(1)}, u32[]{:S(2)}, u32[]{:S(2)}) collective-permute-start(f32[4,80,512]{2,1,0:T(8,128)} %get-tuple-element.13), channel_id=1, source_target_pairs={{0,127},{1,2},{2,1},{3,4},{4,3},{5,6},{6,5},{7,8},{8,7},{9,10},{10... | collective-permute-start | bytes 1966088 | tf_op jit(solution)/shard_map/ppermute | solution.py:462
  17.5 21.0 %copy-start.2 = (s32[1,16]{1,0:T(1,128)S(1)}, s32[1,16]{1,0:T(1,128)}, u32[]{:S(2)}) copy-start(s32[1,16]{1,0:T(1,128)} %param.14) | copy-start | bytes 196
  23.0 31.1 %all-to-all-start = ((f32[128,1,1152]{2,1,0:T(1,128)}), f32[128,1,1152]{2,1,0:T(1,128)}, u32[]{:S(2)}, u32[]{:S(2)}) async-start(f32[128,1,1152]{2,1,0:T(1,128)} %bitcast.9), calls=%async_computation | async-start | bytes 1179648 | tf_op jit(solution)/shard_map/all_to_all | solution.py:467
  37.7 0.8 %copy-start.3 = (f32[4,80,512]{2,1,0:T(8,128)}, f32[4,80,512]{2,1,0:T(8,128)S(1)}, u32[]{:S(2)}) copy-start(f32[4,80,512]{2,1,0:T(8,128)S(1)} %collective-permute-done.1.two_ref) | copy-start | bytes 1966084
  38.5 1.1 %copy-start.4 = (f32[4,80,512]{2,1,0:T(8,128)S(1)}, f32[4,80,512]{2,1,0:T(8,128)}, u32[]{:S(2)}) copy-start(f32[4,80,512]{2,1,0:T(8,128)} %copy-done.3) | copy-start | bytes 1966084
  53.3 0.8 %copy-start = (f32[80,2048]{1,0:T(8,128)}, f32[80,2048]{1,0:T(8,128)S(1)}, u32[]{:S(2)}) copy-start(f32[80,2048]{1,0:T(8,128)S(1)} %get-tuple-element.18._.gain_ref) | copy-start | bytes 1966084
  56.1 4.3 %collective-permute-start.4 = (f32[4,16,128]{2,1,0:T(8,128)}, f32[4,16,128]{2,1,0:T(8,128)S(1)}, u32[]{:S(2)}, u32[]{:S(2)}) collective-permute-start(f32[4,16,128]{2,1,0:T(8,128)} %shard_map.126), channel_id=1, source_target_pairs={{0,128},{128,0},{1,129},{129,1},{2,130},{130,2},{3,131},{131,3},{4... | collective-permute-start | bytes 98312 | tf_op jit(solution)/shard_map/ppermute | solution.py:474
  60.4 1.1 %copy-start.1 = (f32[80,2048]{1,0:T(8,128)S(1)}, f32[80,2048]{1,0:T(8,128)}, u32[]{:S(2)}) copy-start(f32[80,2048]{1,0:T(8,128)} %copy-done) | copy-start | bytes 1966084
where the time goes:
time: 64.7 us; the launch traced here: 64.3 us
  Pallas kernels  27.9 us (43%)
  starting transfers between devices  27 us (42%)
  waiting for transfers between devices  4.77 us (7%)
  local copies, waits for them, and re-layouts  3.87 us (6%)
  between operations  0.81 us (1%)
    pallas_call x1, Pallas kernels, column_part(): pl.pallas_call(column_body, grid=(steps,), in_specs=[whole(x) for x in (o...  13.7 us
    ppermute x1, starting transfers between devices, local(): top_two = lax.ppermute(top_two, axes, second)  11.1 us
    all_to_all x1, starting transfers between devices, local(): lax.all_to_all(outgoing.reshape(group, 1, CHUNK * LANES), axes, split_axi...  10.9 us
    pallas_call x1, Pallas kernels, remap(): pl.pallas_call(remap_body, in_specs=[vspec()] * 2 + [aspec()] * 2 + [vspe...  5.53 us
    unnamed x22, local copies, waits for them, and re-layouts  3.87 us
    ppermute x1, waiting for transfers between devices, local(): two = lax.ppermute(two, axes, second)  3.69 us
    ppermute x1, starting transfers between devices, local(): flux = lax.ppermute(flux, 'comp', [(0, 1), (1, 0)])  3.26 us
    pallas_call x1, Pallas kernels, finish(): pl.pallas_call(finish_body, grid=(steps,), in_specs=[pl.BlockSpec((fields...  2.77 us
  transfers between devices with their start and end apart: 6, of which 2 were waited for; matrix products, arithmetic and copies ran while one was open for 0% of the time, Pallas kernels for 34%

commit v1 on v0

--- a/solution.py
+++ b/solution.py
@@ -59,51 +59,29 @@
     return [pl.multiple_of(jnp.where(even, *pair), LANES) for pair in ((last, 0), (0, last))]
 
 
-def pack_top_body(even_ref, state_ref, one_ref, two_ref, window, sem):
-    loads = [
-        pltpu.make_async_copy(state_ref.at[0, :, pl.ds(0, 8), pl.ds(at, HALO_W)], window.at[i], sem.at[i])
-        for i, at in enumerate(sides(even_ref, state_ref.shape[3]))
-    ]
-    for load in loads:
-        load.start()
-    for i, ref in enumerate((one_ref, two_ref)):
-        loads[i].wait()
-        ref[...] = window[i, :, 0, :]
-
-
-def pack_top(even, state):
-    fields = state.shape[1]
-    return pl.pallas_call(
-        pack_top_body,
-        in_specs=[sspec(), aspec()],
-        out_specs=[vspec()] * 2,
-        out_shape=[jax.ShapeDtypeStruct((fields, HALO_W), F32)] * 2,
-        scratch_shapes=[pltpu.VMEM((2, fields, 8, HALO_W), F32), pltpu.SemaphoreType.DMA((2,))],
-        cost_estimate=pl.CostEstimate(flops=0, bytes_accessed=10**5, transcendentals=0),
-    )(even, hbm(state))
-
-
-def pack_body(even_ref, state_ref, _, one_ref, two_ref, sem):
+def pack_body(even_ref, state_ref, top_one, top_two, one_ref, two_ref, sem):
     loads = [
         pltpu.make_async_copy(state_ref.at[0, :, :, pl.ds(at, HALO_W)], ref, sem.at[i])
         for i, (at, ref) in enumerate(zip(sides(even_ref, state_ref.shape[3]), (one_ref, two_ref)))
     ]
     for load in loads:
         load.start()
-    for load in loads:
+    for load, ref, top in zip(loads, (one_ref, two_ref), (top_one, top_two)):
         load.wait()
-
-
-def pack(even, state, after):
+        top[...] = ref[:, 0, :]
+
+
+def pack(even, state):
     _, fields, levels, _ = state.shape
+    shape = jax.ShapeDtypeStruct
     return pl.pallas_call(
         pack_body,
-        in_specs=[sspec(), aspec(), pl.BlockSpec(memory_space=pl.ANY)],
-        out_specs=[vspec()] * 2,
-        out_shape=[jax.ShapeDtypeStruct((fields, levels, HALO_W), F32)] * 2,
+        in_specs=[sspec(), aspec()],
+        out_specs=[vspec()] * 4,
+        out_shape=[shape((fields, HALO_W), F32)] * 2 + [shape((fields, levels, HALO_W), F32)] * 2,
         scratch_shapes=[pltpu.SemaphoreType.DMA((2,))],
-        cost_estimate=pl.CostEstimate(flops=0, bytes_accessed=3 * 10**6, transcendentals=0),
-    )(even, hbm(state), after)
+        cost_estimate=pl.CostEstimate(flops=6 * 10**10, bytes_accessed=3 * 10**6, transcendentals=0),
+    )(even, hbm(state))
 
 
 def gather_halo(pick, index, coef):
@@ -123,7 +101,7 @@
 
 def remap_body(
     one_ref, two_ref, state_ref, ops_ref, local_ref, halo_ref, coef_ref, src_ref, owner_ref, tile_ref, weight_ref,
-    star_ref, total_ref, out_ref, window, ops, weights, first_s, second_s, pairs, products, sem,
+    star_ref, total_ref, out_ref, window, weights, first_s, second_s, pairs, products, sem,
 ):
     fields, columns = star_ref.shape
     tiles = columns // LANES
@@ -136,9 +114,7 @@
         for i in range(parts)
     ]
     load = pltpu.make_async_copy(state_ref.at[0, :, pl.ds(0, 8), :], window, sem.at[parts])
-    load_ops = pltpu.make_async_copy(ops_ref, ops, sem.at[parts + 1])
     load.start()
-    load_ops.start()
     for copy in copies:
         copy.start()
 
@@ -169,11 +145,10 @@
     )
     spread = sum(mm(part, hot) for part in split3(wide))
     load.wait()
-    load_ops.wait()
     for tile in range(tiles):
         where = slice(tile * LANES, (tile + 1) * LANES)
         here = window[:, 0, where]
-        mixed = jnp.dot(here, ops[tile], precision=lax.Precision.HIGHEST, preferred_element_type=F32)
+        mixed = jnp.dot(here, ops_ref[tile], precision=lax.Precision.HIGHEST, preferred_element_type=F32)
         base = tile * (fields + 1)
         total = spread[base + fields : base + fields + 1]
         total_ref[:, where] = jnp.broadcast_to(total, (total_ref.shape[0], LANES))
@@ -224,7 +199,7 @@
     fold = lambda x: x.reshape(blocks, LANES)
     return pl.pallas_call(
         remap_body,
-        in_specs=[vspec()] * 2 + [aspec()] * 2 + [vspec()] * 3 + [sspec(), vspec(), vspec(), aspec()],
+        in_specs=[vspec()] * 2 + [aspec()] + [vspec()] * 4 + [sspec(), vspec(), vspec(), aspec()],
         out_specs=[vspec()] * 3,
         out_shape=[
             jax.ShapeDtypeStruct((fields, columns), F32),
@@ -233,27 +208,27 @@
         ],
         scratch_shapes=[
             pltpu.VMEM((fields, 8, columns), F32),
-            pltpu.VMEM(ops.shape, F32),
             pltpu.VMEM(weight.shape, BF16),
             pltpu.VMEM((tiles, 2 * fields, LANES), F32),
             pltpu.VMEM((tiles, 2 * fields, LANES), F32),
             pltpu.VMEM((remaps // 2, 2 * fields, 2 * LANES), F32),
             pltpu.VMEM((remaps * fields, LANES), F32),
-            pltpu.SemaphoreType.DMA((6,)),
+            pltpu.SemaphoreType.DMA((5,)),
         ],
         compiler_params=params(16),
         cost_estimate=pl.CostEstimate(flops=6 * 10**10, bytes_accessed=6 * 10**6, transcendentals=0),
     )(
-        one, two, hbm(state), hbm(ops), fold(edge_local), fold(edge_halo), fold(edge_coef), src,
+        one, two, hbm(state), ops, fold(edge_local), fold(edge_halo), fold(edge_coef), src,
         owners.reshape(1, remaps), wanted.reshape(1, remaps), hbm(weight),
     )
 
 
 def column_body(
     one_ref, two_ref, local_ref, halo_ref, coef_ref, state_ref, ops_ref, total_ref, star_ref, kappa_ref,
-    active_ref, base_ref, gain_ref, flow_hi, flow_lo, work, inv, up, down,
+    active_ref, base_ref, gain_ref, token_ref, flow_hi, flow_lo, work, inv, up, down,
 ):
     step = pl.program_id(0)
+    token_ref[...] = jnp.zeros_like(token_ref)
     _, fields, levels, width = state_ref.shape
     rows = fields * levels
     per = HALO_W // LANES
@@ -268,10 +243,16 @@
             ref = one_ref if h < per else two_ref
             return ref[:, :, where].reshape(rows, LANES)
 
-        for k in range(blocks):
-            hi, lo = split2(gather_halo(pick, halo_ref[k : k + 1, :], coef_ref[k : k + 1, :]))
-            flow_hi[:, k * LANES : (k + 1) * LANES] = hi
-            flow_lo[:, k * LANES : (k + 1) * LANES] = lo
+        down_h = lax.broadcasted_iota(jnp.int32, (2 * HALO_W, LANES), 0)
+        parts = split2(jnp.concatenate([pick(h) for h in range(2 * per)], axis=1))
+        for k in range(0, blocks, 2):
+            rows_k = [slice(k + j, k + j + 1) for j in range(2)]
+            here = [jnp.where(down_h == halo_ref[row, :], 1.0, 0.0).astype(BF16) for row in rows_k]
+            here = jnp.concatenate(here, axis=1)
+            coef = jnp.concatenate([coef_ref[row, :] for row in rows_k], axis=1)
+            hi, lo = split2((mm(parts[0], here) + mm(parts[1], here)) * coef)
+            flow_hi[:, k * LANES : (k + 2) * LANES] = hi
+            flow_lo[:, k * LANES : (k + 2) * LANES] = lo
 
     across = jnp.transpose(local_ref[...] - step * width)
     lane = lax.broadcasted_iota(jnp.int32, (LANES, LANES), 1)
@@ -283,9 +264,9 @@
     extra = mm(flow_hi[...], hot) + mm(flow_lo[...], hot)
     for tile in tiles:
         here = state_ref[0, :, :, cut[tile]].reshape(rows, LANES)
-        a_hi, a_lo = split2(here)
-        b_hi, b_lo = split2(ops_ref[tile])
-        mixed = mm(a_hi, b_hi) + (mm(a_hi, b_lo) + mm(a_lo, b_hi))
+        both = jnp.concatenate(split2(ops_ref[tile]), axis=1)
+        mixed = mm(jnp.concatenate(split2(here), axis=1), jnp.concatenate([both, both], axis=0))
+        mixed = mixed[:, :LANES] + mixed[:, LANES:]
         work[tile] = here + STEP * ((mixed - here * total_ref[0:1, cut[tile]]) + extra[:, cut[tile]])
 
     depth = lax.broadcasted_iota(jnp.int32, (levels, LANES), 0)
@@ -356,10 +337,15 @@
             pl.BlockSpec((1, levels, width), lambda i: (0, 0, i)),
             sspec(),
         ],
-        out_specs=[pl.BlockSpec((fields, levels, width), lambda i: (0, 0, i)), column],
+        out_specs=[
+            pl.BlockSpec((fields, levels, width), lambda i: (0, 0, i)),
+            column,
+            pl.BlockSpec((8, LANES), lambda i: (0, 0)),
+        ],
         out_shape=[
             jax.ShapeDtypeStruct((fields, levels, columns), F32),
             jax.ShapeDtypeStruct((levels, columns), F32),
+            jax.ShapeDtypeStruct((8, LANES), F32),
         ],
         scratch_shapes=[
             pltpu.VMEM((fields * levels, edges), BF16),
@@ -371,7 +357,7 @@
         ],
         compiler_params=params(24),
         cost_estimate=pl.CostEstimate(flops=6 * 10**10, bytes_accessed=10**7, transcendentals=0),
-    )(one, two, *lists, hbm(state), hbm(ops), total, star, hbm(kappa), active)
+    )(hbm(one), hbm(two), *lists, hbm(state), hbm(ops), total, star, hbm(kappa), active)
 
 
 def gather_body(arrived_ref, _, flux_ref):
@@ -396,46 +382,50 @@
         out_specs=vspec(),
         out_shape=jax.ShapeDtypeStruct((fields, tiles, LANES), F32),
         cost_estimate=pl.CostEstimate(flops=10**6, bytes_accessed=10**6, transcendentals=0),
-    )(arrived, after)
-
-
-def finish_body(base_ref, gain_ref, flux_ref, active_ref, out_ref, flux_out):
-    step = pl.program_id(0)
-    fields, levels, width = base_ref.shape
+    )(hbm(arrived), after)
+
+
+def finish_body(base_ref, gain_ref, flux_ref, active_ref, out_ref, flux_out, result, sem):
+    fields, levels, columns = base_ref.shape
+    steps = result.shape[0]
+    width = columns // steps
+    stores = [
+        pltpu.make_async_copy(result.at[i], out_ref.at[0, :, :, pl.ds(i * width, width)], sem.at[i])
+        for i in range(steps)
+    ]
     depth = lax.broadcasted_iota(jnp.int32, (levels, LANES), 0)
-    for tile in range(width // LANES):
-        where = slice(tile * LANES, (tile + 1) * LANES)
-        place = step * (width // LANES) + tile
-        inside = depth < active_ref[place]
-        gain = gain_ref[:, where]
-        for field in range(fields):
-            flux = flux_ref[field, pl.ds(place, 1), :]
-            flux_out[0, field : field + 1, where] = flux
-            out_ref[0, field, :, where] = jnp.where(inside, base_ref[field, :, where] + gain * flux, 0.0)
+    for i in range(steps):
+        for tile in range(width // LANES):
+            place = i * (width // LANES) + tile
+            whole = slice(place * LANES, (place + 1) * LANES)
+            where = slice(tile * LANES, (tile + 1) * LANES)
+            inside = depth < active_ref[place]
+            gain = gain_ref[:, whole]
+            for field in range(fields):
+                flux = flux_ref[field, place : place + 1, :]
+                flux_out[0, field : field + 1, whole] = flux
+                result[i, field, :, where] = jnp.where(inside, base_ref[field, :, whole] + gain * flux, 0.0)
+        stores[i].start()
+    for store in stores:
+        store.wait()
 
 
 def finish(base, gain, flux, active):
     fields, levels, columns = base.shape
     steps = 4
-    width = columns // steps
     return pl.pallas_call(
         finish_body,
-        grid=(steps,),
-        in_specs=[
-            pl.BlockSpec((fields, levels, width), lambda i: (0, 0, i)),
-            pl.BlockSpec((levels, width), lambda i: (0, i)),
-            pl.BlockSpec(flux.shape, lambda i: (0, 0, 0)),
-            sspec(),
-        ],
-        out_specs=[
-            pl.BlockSpec((1, fields, levels, width), lambda i: (0, 0, 0, i)),
-            pl.BlockSpec((1, fields, width), lambda i: (0, 0, i)),
-        ],
+        in_specs=[vspec(), vspec(), vspec(), sspec()],
+        out_specs=[aspec(), vspec()],
         out_shape=[
             jax.ShapeDtypeStruct((1, fields, levels, columns), F32),
             jax.ShapeDtypeStruct((1, fields, columns), F32),
         ],
-        compiler_params=params(24),
+        scratch_shapes=[
+            pltpu.VMEM((steps, fields, levels, columns // steps), F32),
+            pltpu.SemaphoreType.DMA((steps,)),
+        ],
+        compiler_params=params(16),
         cost_estimate=pl.CostEstimate(flops=10**7, bytes_accessed=6 * 10**6, transcendentals=0),
     )(base, gain, flux, active)
 
@@ -454,8 +444,7 @@
     count = active.reshape(tiles)
     halo = jnp.bitwise_xor(edge_halo, HALO_W * even[0])
 
-    top_one, top_two = pack_top(even, state)
-    one, two = pack(even, state, top_one)
+    top_one, top_two, one, two = pack(even, state)
     top_one = lax.ppermute(top_one, axes, first)
     top_two = lax.ppermute(top_two, axes, second)
     one = lax.ppermute(one, axes, first)
@@ -467,10 +456,10 @@
     arrived = lax.all_to_all(
         outgoing.reshape(group, 1, CHUNK * LANES), axes, split_axis=0, concat_axis=0, tiled=True
     )
-    base, gain = column_part(
+    base, gain, token = column_part(
         one, two, edge_local, halo, edge_coef, state, tile_ops[0], total, star0, kappa, count
     )
-    flux = gather_flux(arrived.reshape(group * CHUNK, LANES), gain, fields, tiles)
+    flux = gather_flux(arrived.reshape(group * CHUNK, LANES), token, fields, tiles)
     flux = lax.ppermute(flux, "comp", [(0, 1), (1, 0)])
     return finish(base, gain, flux, count)
 

time: 64.7 us -> 61 us (0.943)
  Pallas kernels: 27.9 us -> 25.1 us
  local copies, waits for them, and re-layouts: 3.87 us -> 1.47 us
  starting transfers between devices: 27 us -> 28.3 us
    unnamed x22, local copies, waits for them, and re-layouts: 3.87 us -> 1.47 us
    ppermute x1, starting transfers between devices: 0.01 us -> 2.21 us  [local(): top_one = lax.ppermute(top_one, axes, first)]
    pallas_call x4 -> x3, Pallas kernels: 12.2 us -> 10.4 us  [the longest x1 5.15 us: remap(): pl.pallas_call(remap_body, in_specs=[vspec()] * 2 + [aspec()] + [vspec()]...]
    ppermute x1, starting transfers between devices: 11.1 us -> 9.39 us  [local(): top_two = lax.ppermute(top_two, axes, second)]
    ppermute x1, starting transfers between devices: 1.55 us -> 0.01 us  [local(): one = lax.ppermute(one, axes, first)]
    ppermute x1, starting transfers between devices: 3.26 us -> 4.68 us  [local(): flux = lax.ppermute(flux, 'comp', [(0, 1), (1, 0)])]
    pallas_call x1, Pallas kernels: 13.7 us -> 12.7 us  [column_part(): pl.pallas_call(column_body, grid=(steps,), in_specs=[whole(x) for x in (o...]
    ppermute x1, starting transfers between devices: 0.1 us -> 1 us  [local(): two = lax.ppermute(two, axes, second)]
  transfers between devices with their start and end apart: 6 -> 6, of which waited for: 2 -> 4; matrix products, arithmetic and copies ran while one was open for 0% -> 0% of each run, Pallas kernels for 34% -> 29%
where the time goes in v1:
time: 61 us; the launch traced here: 60.7 us
  starting transfers between devices  28.3 us (46%)
  Pallas kernels  25.1 us (41%)
  waiting for transfers between devices  5.1 us (8%)
  local copies, waits for them, and re-layouts  1.47 us (2%)
  between operations  0.8 us (1%)
    pallas_call x1, Pallas kernels, column_part(): pl.pallas_call(column_body, grid=(steps,), in_specs=[whole(x) for x in (o...  12.7 us
    all_to_all x1, starting transfers between devices, local(): lax.all_to_all(outgoing.reshape(group, 1, CHUNK * LANES), axes, split_axi...  11 us
    ppermute x1, starting transfers between devices, local(): top_two = lax.ppermute(top_two, axes, second)  9.39 us
    pallas_call x1, Pallas kernels, remap(): pl.pallas_call(remap_body, in_specs=[vspec()] * 2 + [aspec()] + [vspec()]...  5.15 us
    ppermute x1, starting transfers between devices, local(): flux = lax.ppermute(flux, 'comp', [(0, 1), (1, 0)])  4.68 us
    ppermute x1, waiting for transfers between devices, local(): two = lax.ppermute(two, axes, second)  3.13 us
    pallas_call x1, Pallas kernels, finish(): pl.pallas_call(finish_body, in_specs=[vspec(), vspec(), vspec(), sspec()]...  2.79 us
    pallas_call x1, Pallas kernels, pack(): pl.pallas_call(pack_body, in_specs=[sspec(), aspec()], out_specs=[vspec()...  2.45 us
  transfers between devices with their start and end apart: 6, of which 4 were waited for; matrix products, arithmetic and copies ran while one was open for 0% of the time, Pallas kernels for 29%

profile of v1, /device:TPU:1, one launch (start us, length us, event | category | flops | bytes accessed | tf_op | source)
XLA Modules:
  0.0 60.7 jit_solution(6126674184359423317)
XLA Ops:
  0.6 0.0 copy-start.8
  0.7 0.0 copy-start.2
  0.7 0.0 copy-start.3
  0.7 0.0 copy-start.4
  0.7 0.0 copy-start.5
  0.7 0.0 copy-start.6
  0.7 0.0 copy-start.7
  0.7 2.4 %shard_map.122 = (f32[4,512]{1,0:T(4,128)}, f32[4,512]{1,0:T(4,128)}, f32[4,80,512]{2,1,0:T(8,128)}, f32[4,80,512]{2,1,0:T(8,128)}) custom-call(s32[1]{0:T(128)} %bitcast.even_ref, f32[1,4,80,2048]{3,2,1,0:T(8,128)} %state_ref.5), custom_call_target="tpu_custom_call" | custom-call | flops 60000002048 | bytes 3000000 | tf_op jit(solution)/shard_map/pallas_call | solution.py:77
  3.2 2.2 %collective-permute-start.2 = (f32[4,512]{1,0:T(4,128)}, f32[4,512]{1,0:T(4,128)S(1)}, u32[]{:S(2)}, u32[]{:S(2)}) collective-permute-start(f32[4,512]{1,0:T(4,128)} %get-tuple-element.14), channel_id=1, source_target_pairs={{0,1},{1,0},{2,3},{3,2},{4,5},{5,4},{6,7},{7,6},{8,9},{9,8},{10,11... | collective-permute-start | bytes 24584 | tf_op jit(solution)/shard_map/ppermute | solution.py:448
  5.4 9.4 %collective-permute-start.3 = (f32[4,512]{1,0:T(4,128)}, f32[4,512]{1,0:T(4,128)S(1)}, u32[]{:S(2)}, u32[]{:S(2)}) collective-permute-start(f32[4,512]{1,0:T(4,128)} %get-tuple-element.15), channel_id=1, source_target_pairs={{0,127},{1,2},{2,1},{3,4},{4,3},{5,6},{6,5},{7,8},{8,7},{9,10},{10... | collective-permute-start | bytes 24584 | tf_op jit(solution)/shard_map/ppermute | solution.py:449
  14.8 0.0 collective-permute-start
  14.8 1.0 %collective-permute-start.1 = (f32[4,80,512]{2,1,0:T(8,128)}, f32[4,80,512]{2,1,0:T(8,128)S(1)}, u32[]{:S(2)}, u32[]{:S(2)}) collective-permute-start(f32[4,80,512]{2,1,0:T(8,128)} %get-tuple-element.13), channel_id=1, source_target_pairs={{0,127},{1,2},{2,1},{3,4},{4,3},{5,6},{6,5},{7,8},{8,7},{9,10},{10... | collective-permute-start | bytes 1966088 | tf_op jit(solution)/shard_map/ppermute | solution.py:451
  15.8 0.0 copy-done.8
  15.8 0.0 collective-permute-done.2.one_ref
  15.8 0.2 collective-permute-done.3.two_ref
  16.0 0.0 copy-done.2
  16.1 0.0 copy-start.1
  16.1 5.2 %shard_map.123 = (f32[4,2048]{1,0:T(4,128)S(1)}, f32[8,2048]{1,0:T(8,128)S(1)}, f32[1152,128]{1,0:T(8,128)}) custom-call(f32[4,512]{1,0:T(4,128)S(1)} %collective-permute-done.2.one_ref, f32[4,512]{1,0:T(4,128)S(1)} %collective-permute-done.3.two_ref, f32[1,4,80,2048]{3,2,1,0:T(8,128)} %state_ref.5, f32[16,128,128]{2,1,0:T(8,128)S(1)} %bitcast.16, ...), custom_call_target="tpu_custom_call" | custom-call | flops 60000002048 | bytes 6000000 | tf_op jit(solution)/shard_map/pallas_call | solution.py:200
  21.2 11.0 %all-to-all-start = ((f32[128,1,1152]{2,1,0:T(1,128)}), f32[128,1,1152]{2,1,0:T(1,128)}, u32[]{:S(2)}, u32[]{:S(2)}) async-start(f32[128,1,1152]{2,1,0:T(1,128)} %bitcast.9), calls=%async_computation | async-start | bytes 1179648 | tf_op jit(solution)/shard_map/all_to_all | solution.py:456
  32.2 0.0 collective-permute-done.one_ref
  32.3 0.0 copy-start.9
  32.3 3.1 %collective-permute-done.1.two_ref = f32[4,80,512]{2,1,0:T(8,128)S(1)} collective-permute-done((f32[4,80,512]{2,1,0:T(8,128)}, f32[4,80,512]{2,1,0:T(8,128)S(1)}, u32[]{:S(2)}, u32[]{:S(2)}) %collective-permute-start.1) | collective-permute-done | bytes 655392 | tf_op jit(solution)/shard_map/ppermute | solution.py:451
  35.4 0.8 %copy-done.10 = f32[4,80,512]{2,1,0:T(8,128)} copy-done((f32[4,80,512]{2,1,0:T(8,128)}, f32[4,80,512]{2,1,0:T(8,128)S(1)}, u32[]{:S(2)}) %copy-start.10) | copy-done | bytes 655384
  36.2 0.0 copy-done.1
  36.3 12.7 %shard_map.124 = (f32[4,80,2048]{2,1,0:T(8,128)S(1)}, f32[80,2048]{1,0:T(8,128)S(1)}, f32[8,128]{1,0:T(8,128)S(1)}) custom-call(f32[4,80,512]{2,1,0:T(8,128)} %copy-done.9, f32[4,80,512]{2,1,0:T(8,128)} %copy-done.10, s32[8,128]{1,0:T(8,128)S(1)} %bitcast.18, s32[8,128]{1,0:T(8,128)S(1)} %bitcast.12, f32[8,128]{1,0:T(8,128)S(1)} %bitcast.20, ...), custom_call_target="tpu_custom_call" | custom-call | flops 60000002048 | bytes 10000000 | tf_op jit(solution)/shard_map/pallas_call | solution.py:328
  49.0 0.0 copy-start
  49.0 0.6 copy-done
  49.6 0.7 %all-to-all-done = f32[128,1,1152]{2,1,0:T(1,128)} async-done(((f32[128,1,1152]{2,1,0:T(1,128)}), f32[128,1,1152]{2,1,0:T(1,128)}, u32[]{:S(2)}, u32[]{:S(2)}) %all-to-all-start) | async-done | bytes 589856 | tf_op jit(solution)/shard_map/all_to_all | solution.py:456
  50.2 2.0 %shard_map.125 = f32[4,16,128]{2,1,0:T(8,128)} custom-call(f32[1152,128]{1,0:T(8,128)} %bitcast.10.arrived_ref, f32[8,128]{1,0:T(8,128)} %copy-done), custom_call_target="tpu_custom_call" | custom-call | flops 1000000 | bytes 1000000 | tf_op jit(solution)/shard_map/pallas_call | solution.py:379
  52.2 4.7 %collective-permute-start.4 = (f32[4,16,128]{2,1,0:T(8,128)}, f32[4,16,128]{2,1,0:T(8,128)S(1)}, u32[]{:S(2)}, u32[]{:S(2)}) collective-permute-start(f32[4,16,128]{2,1,0:T(8,128)} %shard_map.125), channel_id=1, source_target_pairs={{0,128},{128,0},{1,129},{129,1},{2,130},{130,2},{3,131},{131,3},{4... | collective-permute-start | bytes 98312 | tf_op jit(solution)/shard_map/ppermute | solution.py:463
  56.9 1.1 %collective-permute-done.4.flux_ref = f32[4,16,128]{2,1,0:T(8,128)S(1)} collective-permute-done((f32[4,16,128]{2,1,0:T(8,128)}, f32[4,16,128]{2,1,0:T(8,128)S(1)}, u32[]{:S(2)}, u32[]{:S(2)}) %collective-permute-start.4) | collective-permute-done | bytes 32800 | tf_op jit(solution)/shard_map/ppermute | solution.py:463
  57.9 2.8 %shard_map.126 = (f32[1,4,80,2048]{3,2,1,0:T(8,128)}, f32[1,4,2048]{2,1,0:T(4,128)}) custom-call(f32[4,80,2048]{2,1,0:T(8,128)S(1)} %get-tuple-element.18.base_ref, f32[80,2048]{1,0:T(8,128)S(1)} %get-tuple-element.19.gain_ref, f32[4,16,128]{2,1,0:T(8,128)S(1)} %collective-permute-done.4.flux_ref, s32[16]{0:T(128)S(1)} %bitcast.14), custom_call_target="tpu_custom_call" | custom-call | flops 10000000 | bytes 6000000 | tf_op jit(solution)/shard_map/pallas_call | solution.py:416
  (8 shorter events, 0.0 us)
Async XLA Ops:
  0.6 15.1 %copy-start.8 = (s32[1,1024]{1,0:T(1,128)S(1)}, s32[1,1024]{1,0:T(1,128)}, u32[]{:S(2)}) copy-start(s32[1,1024]{1,0:T(1,128)} %param.16) | copy-start | bytes 12292
  0.7 15.4 %copy-start.2 = (f32[1,16,128,128]{3,2,1,0:T(8,128)S(1)}, f32[1,16,128,128]{3,2,1,0:T(8,128)}, u32[]{:S(2)}) copy-start(f32[1,16,128,128]{3,2,1,0:T(8,128)} %param.12) | copy-start | bytes 3145732
  0.7 15.4 %copy-start.3 = (s32[1,1024]{1,0:T(1,128)S(1)}, s32[1,1024]{1,0:T(1,128)}, u32[]{:S(2)}) copy-start(s32[1,1024]{1,0:T(1,128)} %param.15) | copy-start | bytes 12292
  0.7 15.4 %copy-start.4 = (f32[1,1024]{1,0:T(1,128)S(1)}, f32[1,1024]{1,0:T(1,128)}, u32[]{:S(2)}) copy-start(f32[1,1024]{1,0:T(1,128)} %param.17) | copy-start | bytes 12292
  0.7 15.3 %copy-start.5 = (s32[1,128]{1,0:T(1,128)S(1)}, s32[1,128]{1,0:T(1,128)}, u32[]{:S(2)}) copy-start(s32[1,128]{1,0:T(1,128)} %param.18) | copy-start | bytes 1540
  0.7 15.3 %copy-start.6 = (s32[1,128,1]{1,2,0:T(1,128)S(1)}, s32[1,128,1]{1,2,0:T(1,128)}, u32[]{:S(2)}) copy-start(s32[1,128,1]{1,2,0:T(1,128)} %param.19) | copy-start | bytes 1540
  0.7 15.3 %copy-start.7 = (s32[1,128]{1,0:T(1,128)S(1)}, s32[1,128]{1,0:T(1,128)}, u32[]{:S(2)}) copy-start(s32[1,128]{1,0:T(1,128)} %tile_ref.1) | copy-start | bytes 1540
  3.2 12.6 %collective-permute-start.2 = (f32[4,512]{1,0:T(4,128)}, f32[4,512]{1,0:T(4,128)S(1)}, u32[]{:S(2)}, u32[]{:S(2)}) collective-permute-start(f32[4,512]{1,0:T(4,128)} %get-tuple-element.14), channel_id=1, source_target_pairs={{0,1},{1,0},{2,3},{3,2},{4,5},{5,4},{6,7},{7,6},{8,9},{9,8},{10,11... | collective-permute-start | bytes 24584 | tf_op jit(solution)/shard_map/ppermute | solution.py:448
  5.4 10.6 %collective-permute-start.3 = (f32[4,512]{1,0:T(4,128)}, f32[4,512]{1,0:T(4,128)S(1)}, u32[]{:S(2)}, u32[]{:S(2)}) collective-permute-start(f32[4,512]{1,0:T(4,128)} %get-tuple-element.15), channel_id=1, source_target_pairs={{0,127},{1,2},{2,1},{3,4},{4,3},{5,6},{6,5},{7,8},{8,7},{9,10},{10... | collective-permute-start | bytes 24584 | tf_op jit(solution)/shard_map/ppermute | solution.py:449
  14.8 17.5 %collective-permute-start = (f32[4,80,512]{2,1,0:T(8,128)}, f32[4,80,512]{2,1,0:T(8,128)S(1)}, u32[]{:S(2)}, u32[]{:S(2)}) collective-permute-start(f32[4,80,512]{2,1,0:T(8,128)} %get-tuple-element.12), channel_id=1, source_target_pairs={{0,1},{1,0},{2,3},{3,2},{4,5},{5,4},{6,7},{7,6},{8,9},{9,8},{10,11... | collective-permute-start | bytes 1966088 | tf_op jit(solution)/shard_map/ppermute | solution.py:450
  14.8 20.6 %collective-permute-start.1 = (f32[4,80,512]{2,1,0:T(8,128)}, f32[4,80,512]{2,1,0:T(8,128)S(1)}, u32[]{:S(2)}, u32[]{:S(2)}) collective-permute-start(f32[4,80,512]{2,1,0:T(8,128)} %get-tuple-element.13), channel_id=1, source_target_pairs={{0,127},{1,2},{2,1},{3,4},{4,3},{5,6},{6,5},{7,8},{8,7},{9,10},{10... | collective-permute-start | bytes 1966088 | tf_op jit(solution)/shard_map/ppermute | solution.py:451
  16.1 20.2 %copy-start.1 = (s32[1,16]{1,0:T(1,128)S(1)}, s32[1,16]{1,0:T(1,128)}, u32[]{:S(2)}) copy-start(s32[1,16]{1,0:T(1,128)} %param.14) | copy-start | bytes 196
  21.2 29.0 %all-to-all-start = ((f32[128,1,1152]{2,1,0:T(1,128)}), f32[128,1,1152]{2,1,0:T(1,128)}, u32[]{:S(2)}, u32[]{:S(2)}) async-start(f32[128,1,1152]{2,1,0:T(1,128)} %bitcast.9), calls=%async_computation | async-start | bytes 1179648 | tf_op jit(solution)/shard_map/all_to_all | solution.py:456
  32.3 3.1 %copy-start.9 = (f32[4,80,512]{2,1,0:T(8,128)}, f32[4,80,512]{2,1,0:T(8,128)S(1)}, u32[]{:S(2)}) copy-start(f32[4,80,512]{2,1,0:T(8,128)S(1)} %collective-permute-done.one_ref) | copy-start | bytes 1966084
  35.4 0.8 %copy-start.10 = (f32[4,80,512]{2,1,0:T(8,128)}, f32[4,80,512]{2,1,0:T(8,128)S(1)}, u32[]{:S(2)}) copy-start(f32[4,80,512]{2,1,0:T(8,128)S(1)} %collective-permute-done.1.two_ref) | copy-start | bytes 1966084
  49.0 0.6 copy-start
  52.2 5.7 %collective-permute-start.4 = (f32[4,16,128]{2,1,0:T(8,128)}, f32[4,16,128]{2,1,0:T(8,128)S(1)}, u32[]{:S(2)}, u32[]{:S(2)}) collective-permute-start(f32[4,16,128]{2,1,0:T(8,128)} %shard_map.125), channel_id=1, source_target_pairs={{0,128},{128,0},{1,129},{129,1},{2,130},{130,2},{3,131},{131,3},{4... | collective-permute-start | bytes 98312 | tf_op jit(solution)/shard_map/ppermute | solution.py:463

commit v2 on v1

--- a/solution.py
+++ b/solution.py
@@ -345,7 +345,7 @@
         out_shape=[
             jax.ShapeDtypeStruct((fields, levels, columns), F32),
             jax.ShapeDtypeStruct((levels, columns), F32),
-            jax.ShapeDtypeStruct((8, LANES), F32),
+            pltpu.HBM((8, LANES), F32),
         ],
         scratch_shapes=[
             pltpu.VMEM((fields * levels, edges), BF16),
@@ -360,32 +360,7 @@
     )(hbm(one), hbm(two), *lists, hbm(state), hbm(ops), total, star, hbm(kappa), active)
 
 
-def gather_body(arrived_ref, _, flux_ref):
-    fields, tiles, _ = flux_ref.shape
-    sources = arrived_ref.shape[0] // CHUNK
-    labels = jnp.transpose(arrived_ref[pl.ds(2 * fields, sources, stride=CHUNK), :])
-    tile = lax.broadcasted_iota(jnp.int32, (tiles, sources), 0).astype(F32)
-    select = jnp.concatenate(
-        [jnp.where(tile == labels[k : k + 1, :], 1.0, 0.0).astype(BF16) for k in range(2)], axis=1
-    )
-    for field in range(fields):
-        value = jnp.concatenate(
-            [arrived_ref[pl.ds(k * fields + field, sources, stride=CHUNK), :] for k in range(2)], axis=0
-        )
-        flux_ref[field] = sum(mm(select, part) for part in split3(value))
-
-
-def gather_flux(arrived, after, fields, tiles):
-    return pl.pallas_call(
-        gather_body,
-        in_specs=[vspec(), pl.BlockSpec(memory_space=pl.ANY)],
-        out_specs=vspec(),
-        out_shape=jax.ShapeDtypeStruct((fields, tiles, LANES), F32),
-        cost_estimate=pl.CostEstimate(flops=10**6, bytes_accessed=10**6, transcendentals=0),
-    )(hbm(arrived), after)
-
-
-def finish_body(base_ref, gain_ref, flux_ref, active_ref, out_ref, flux_out, result, sem):
+def finish_body(base_ref, gain_ref, arrived_ref, active_ref, out_ref, flux_out, flux_ref, result, sem):
     fields, levels, columns = base_ref.shape
     steps = result.shape[0]
     width = columns // steps
@@ -393,6 +368,18 @@
         pltpu.make_async_copy(result.at[i], out_ref.at[0, :, :, pl.ds(i * width, width)], sem.at[i])
         for i in range(steps)
     ]
+    tiles = columns // LANES
+    sources = arrived_ref.shape[0] // CHUNK
+    labels = jnp.transpose(arrived_ref[pl.ds(2 * fields, sources, stride=CHUNK), :])
+    named = lax.broadcasted_iota(jnp.int32, (tiles, sources), 0).astype(F32)
+    select = jnp.concatenate(
+        [jnp.where(named == labels[k : k + 1, :], 1.0, 0.0).astype(BF16) for k in range(2)], axis=1
+    )
+    for field in range(fields):
+        value = jnp.concatenate(
+            [arrived_ref[pl.ds(k * fields + field, sources, stride=CHUNK), :] for k in range(2)], axis=0
+        )
+        flux_ref[field] = sum(mm(select, part) for part in split3(value))
     depth = lax.broadcasted_iota(jnp.int32, (levels, LANES), 0)
     for i in range(steps):
         for tile in range(width // LANES):
@@ -410,7 +397,7 @@
         store.wait()
 
 
-def finish(base, gain, flux, active):
+def finish(base, gain, arrived, active):
     fields, levels, columns = base.shape
     steps = 4
     return pl.pallas_call(
@@ -422,12 +409,29 @@
             jax.ShapeDtypeStruct((1, fields, columns), F32),
         ],
         scratch_shapes=[
+            pltpu.VMEM((fields, columns // LANES, LANES), F32),
             pltpu.VMEM((steps, fields, levels, columns // steps), F32),
             pltpu.SemaphoreType.DMA((steps,)),
         ],
         compiler_params=params(16),
         cost_estimate=pl.CostEstimate(flops=10**7, bytes_accessed=6 * 10**6, transcendentals=0),
-    )(base, gain, flux, active)
+    )(base, gain, arrived, active)
+
+
+def after_body(value_ref, token_ref, out_ref):
+    pass
+
+
+def after(value, token):
+    anywhere = pl.BlockSpec(memory_space=pl.ANY)
+    return pl.pallas_call(
+        after_body,
+        in_specs=[anywhere, anywhere],
+        out_specs=anywhere,
+        out_shape=jax.ShapeDtypeStruct(value.shape, value.dtype),
+        input_output_aliases={0: 0},
+        cost_estimate=pl.CostEstimate(flops=0, bytes_accessed=0, transcendentals=0),
+    )(value, token)
 
 
 def local(
@@ -459,9 +463,8 @@
     base, gain, token = column_part(
         one, two, edge_local, halo, edge_coef, state, tile_ops[0], total, star0, kappa, count
     )
-    flux = gather_flux(arrived.reshape(group * CHUNK, LANES), token, fields, tiles)
-    flux = lax.ppermute(flux, "comp", [(0, 1), (1, 0)])
-    return finish(base, gain, flux, count)
+    arrived = lax.ppermute(after(arrived, token), "comp", [(0, 1), (1, 0)])
+    return finish(base, gain, arrived.reshape(group * CHUNK, LANES), count)
 
 
 def solution(mesh):

time: 61 us -> 60.3 us (0.989)
  Pallas kernels: 25.1 us -> 24.2 us
  waiting for transfers between devices: 5.1 us -> 5.88 us
    pallas_call x1, Pallas kernels: 1.95 us -> 0.01 us  [after(): pl.pallas_call(after_body, in_specs=[anywhere, anywhere], out_specs=anywh...]
    ppermute x1, waiting for transfers between devices: 1.07 us -> 1.84 us  [local(): arrived = lax.ppermute(after(arrived, token), 'comp', [(0, 1), (1, 0)])]
    unnamed x22 -> x20, local copies, waits for them, and re-layouts: 1.47 us -> 0.89 us
  transfers between devices with their start and end apart: 6 -> 6, of which waited for: 4 -> 4; matrix products, arithmetic and copies ran while one was open for 0% -> 0% of each run, Pallas kernels for 29% -> 31%
where the time goes in v2:
time: 60.3 us; the launch traced here: 60.1 us
  starting transfers between devices  28.3 us (47%)
  Pallas kernels  24.2 us (40%)
  waiting for transfers between devices  5.88 us (10%)
  local copies, waits for them, and re-layouts  0.89 us (1%)
  between operations  0.79 us (1%)
    pallas_call x1, Pallas kernels, column_part(): pl.pallas_call(column_body, grid=(steps,), in_specs=[whole(x) for x in (o...  13.3 us
    all_to_all x1, starting transfers between devices, local(): lax.all_to_all(outgoing.reshape(group, 1, CHUNK * LANES), axes, split_axi...  11 us
    ppermute x1, starting transfers between devices, local(): top_two = lax.ppermute(top_two, axes, second)  9.39 us
    pallas_call x1, Pallas kernels, remap(): pl.pallas_call(remap_body, in_specs=[vspec()] * 2 + [aspec()] + [vspec()]...  5.16 us
    ppermute x1, starting transfers between devices, local(): arrived = lax.ppermute(after(arrived, token), 'comp', [(0, 1), (1, 0)])  4.68 us
    pallas_call x1, Pallas kernels, finish(): pl.pallas_call(finish_body, in_specs=[vspec(), vspec(), vspec(), sspec()]...  3.29 us
    ppermute x1, waiting for transfers between devices, local(): two = lax.ppermute(two, axes, second)  3.13 us
    pallas_call x1, Pallas kernels, pack(): pl.pallas_call(pack_body, in_specs=[sspec(), aspec()], out_specs=[vspec()...  2.45 us
  transfers between devices with their start and end apart: 6, of which 4 were waited for; matrix products, arithmetic and copies ran while one was open for 0% of the time, Pallas kernels for 31%

profile of v2, /device:TPU:1, one launch (start us, length us, event | category | flops | bytes accessed | tf_op | source)
XLA Modules:
  0.0 60.1 jit_solution(429693878471665616)
XLA Ops:
  0.6 0.0 copy-start.7
  0.7 0.0 copy-start.1
  0.7 0.0 copy-start.2
  0.7 0.0 copy-start.3
  0.7 0.0 copy-start.4
  0.7 0.0 copy-start.5
  0.7 0.0 copy-start.6
  0.7 2.4 %shard_map.122 = (f32[4,512]{1,0:T(4,128)}, f32[4,512]{1,0:T(4,128)}, f32[4,80,512]{2,1,0:T(8,128)}, f32[4,80,512]{2,1,0:T(8,128)}) custom-call(s32[1]{0:T(128)} %bitcast.even_ref, f32[1,4,80,2048]{3,2,1,0:T(8,128)} %state_ref.5), custom_call_target="tpu_custom_call" | custom-call | flops 60000002048 | bytes 3000000 | tf_op jit(solution)/shard_map/pallas_call | solution.py:77
  3.2 2.2 %collective-permute-start.2 = (f32[4,512]{1,0:T(4,128)}, f32[4,512]{1,0:T(4,128)S(1)}, u32[]{:S(2)}, u32[]{:S(2)}) collective-permute-start(f32[4,512]{1,0:T(4,128)} %get-tuple-element.14), channel_id=1, source_target_pairs={{0,1},{1,0},{2,3},{3,2},{4,5},{5,4},{6,7},{7,6},{8,9},{9,8},{10,11... | collective-permute-start | bytes 24584 | tf_op jit(solution)/shard_map/ppermute | solution.py:452
  5.4 9.4 %collective-permute-start.3 = (f32[4,512]{1,0:T(4,128)}, f32[4,512]{1,0:T(4,128)S(1)}, u32[]{:S(2)}, u32[]{:S(2)}) collective-permute-start(f32[4,512]{1,0:T(4,128)} %get-tuple-element.15), channel_id=1, source_target_pairs={{0,127},{1,2},{2,1},{3,4},{4,3},{5,6},{6,5},{7,8},{8,7},{9,10},{10... | collective-permute-start | bytes 24584 | tf_op jit(solution)/shard_map/ppermute | solution.py:453
  14.8 0.0 collective-permute-start
  14.8 1.0 %collective-permute-start.1 = (f32[4,80,512]{2,1,0:T(8,128)}, f32[4,80,512]{2,1,0:T(8,128)S(1)}, u32[]{:S(2)}, u32[]{:S(2)}) collective-permute-start(f32[4,80,512]{2,1,0:T(8,128)} %get-tuple-element.13), channel_id=1, source_target_pairs={{0,127},{1,2},{2,1},{3,4},{4,3},{5,6},{6,5},{7,8},{8,7},{9,10},{10... | collective-permute-start | bytes 1966088 | tf_op jit(solution)/shard_map/ppermute | solution.py:455
  15.8 0.0 copy-done.7
  15.8 0.0 collective-permute-done.2.one_ref
  15.8 0.2 collective-permute-done.3.two_ref
  16.0 0.0 copy-done.1
  16.0 0.0 copy-done.3
  16.0 0.0 copy-done.4
  16.0 0.0 copy-done.5
  16.1 0.0 copy-done.6
  16.1 0.0 copy-start
  16.1 5.2 %shard_map.123 = (f32[4,2048]{1,0:T(4,128)S(1)}, f32[8,2048]{1,0:T(8,128)S(1)}, f32[1152,128]{1,0:T(8,128)}) custom-call(f32[4,512]{1,0:T(4,128)S(1)} %collective-permute-done.2.one_ref, f32[4,512]{1,0:T(4,128)S(1)} %collective-permute-done.3.two_ref, f32[1,4,80,2048]{3,2,1,0:T(8,128)} %state_ref.5, f32[16,128,128]{2,1,0:T(8,128)S(1)} %bitcast.17, ...), custom_call_target="tpu_custom_call" | custom-call | flops 60000002048 | bytes 6000000 | tf_op jit(solution)/shard_map/pallas_call | solution.py:200
  21.2 11.0 %all-to-all-start = ((f32[128,1,1152]{2,1,0:T(1,128)}), f32[128,1,1152]{2,1,0:T(1,128)}, u32[]{:S(2)}, u32[]{:S(2)}) async-start(f32[128,1,1152]{2,1,0:T(1,128)} %bitcast.9), calls=%async_computation | async-start | bytes 1179648 | tf_op jit(solution)/shard_map/all_to_all | solution.py:460
  32.3 0.0 collective-permute-done.one_ref
  32.3 0.0 copy-start.8
  32.3 3.1 %collective-permute-done.1.two_ref = f32[4,80,512]{2,1,0:T(8,128)S(1)} collective-permute-done((f32[4,80,512]{2,1,0:T(8,128)}, f32[4,80,512]{2,1,0:T(8,128)S(1)}, u32[]{:S(2)}, u32[]{:S(2)}) %collective-permute-start.1) | collective-permute-done | bytes 655392 | tf_op jit(solution)/shard_map/ppermute | solution.py:455
  35.4 0.8 %copy-done.9 = f32[4,80,512]{2,1,0:T(8,128)} copy-done((f32[4,80,512]{2,1,0:T(8,128)}, f32[4,80,512]{2,1,0:T(8,128)S(1)}, u32[]{:S(2)}) %copy-start.9) | copy-done | bytes 655384
  36.3 13.3 %shard_map.124 = (f32[4,80,2048]{2,1,0:T(8,128)S(1)}, f32[80,2048]{1,0:T(8,128)S(1)}, f32[8,128]{1,0:T(8,128)}) custom-call(f32[4,80,512]{2,1,0:T(8,128)} %copy-done.8, f32[4,80,512]{2,1,0:T(8,128)} %copy-done.9, s32[8,128]{1,0:T(8,128)S(1)} %bitcast.19, s32[8,128]{1,0:T(8,128)S(1)} %bitcast.13, f32[8,128]{1,0:T(8,128)S(1)} %bitcast.21, ...), custom_call_target="tpu_custom_call" | custom-call | flops 60000002048 | bytes 10000000 | tf_op jit(solution)/shard_map/pallas_call | solution.py:328
  49.6 0.7 %all-to-all-done.value_ref = f32[128,1,1152]{2,1,0:T(1,128)} async-done(((f32[128,1,1152]{2,1,0:T(1,128)}), f32[128,1,1152]{2,1,0:T(1,128)}, u32[]{:S(2)}, u32[]{:S(2)}) %all-to-all-start) | async-done | bytes 589856 | tf_op jit(solution)/shard_map/all_to_all | solution.py:460
  50.2 4.7 %collective-permute-start.4 = (f32[128,1,1152]{2,1,0:T(1,128)}, f32[128,1,1152]{2,1,0:T(1,128)S(1)}, u32[]{:S(2)}, u32[]{:S(2)}) collective-permute-start(f32[128,1,1152]{2,1,0:T(1,128)} %shard_map.125), channel_id=1, source_target_pairs={{0,128},{128,0},{1,129},{129,1},{2,130},{130,2},{3,131},{131,3},{4... | collective-permute-start | bytes 1769480 | tf_op jit(solution)/shard_map/ppermute | solution.py:466
  54.9 1.8 %collective-permute-done.4 = f32[128,1,1152]{2,1,0:T(1,128)S(1)} collective-permute-done((f32[128,1,1152]{2,1,0:T(1,128)}, f32[128,1,1152]{2,1,0:T(1,128)S(1)}, u32[]{:S(2)}, u32[]{:S(2)}) %collective-permute-start.4) | collective-permute-done | bytes 589856 | tf_op jit(solution)/shard_map/ppermute | solution.py:466
  56.8 3.3 %shard_map.126 = (f32[1,4,80,2048]{3,2,1,0:T(8,128)}, f32[1,4,2048]{2,1,0:T(4,128)}) custom-call(f32[4,80,2048]{2,1,0:T(8,128)S(1)} %get-tuple-element.18.base_ref, f32[80,2048]{1,0:T(8,128)S(1)} %get-tuple-element.19.gain_ref, f32[1152,128]{1,0:T(8,128)S(1)} %bitcast.11, s32[16]{0:T(128)S(1)} %bitcast.15), custom_call_target="tpu_custom_call" | custom-call | flops 10000000 | bytes 6000000 | tf_op jit(solution)/shard_map/pallas_call | solution.py:403
  (6 shorter events, 0.0 us)
Async XLA Ops:
  0.6 15.1 %copy-start.7 = (s32[1,1024]{1,0:T(1,128)S(1)}, s32[1,1024]{1,0:T(1,128)}, u32[]{:S(2)}) copy-start(s32[1,1024]{1,0:T(1,128)} %param.16) | copy-start | bytes 12292
  0.7 15.4 %copy-start.1 = (f32[1,16,128,128]{3,2,1,0:T(8,128)S(1)}, f32[1,16,128,128]{3,2,1,0:T(8,128)}, u32[]{:S(2)}) copy-start(f32[1,16,128,128]{3,2,1,0:T(8,128)} %param.12) | copy-start | bytes 3145732
  0.7 15.4 %copy-start.2 = (s32[1,1024]{1,0:T(1,128)S(1)}, s32[1,1024]{1,0:T(1,128)}, u32[]{:S(2)}) copy-start(s32[1,1024]{1,0:T(1,128)} %param.15) | copy-start | bytes 12292
  0.7 15.4 %copy-start.3 = (f32[1,1024]{1,0:T(1,128)S(1)}, f32[1,1024]{1,0:T(1,128)}, u32[]{:S(2)}) copy-start(f32[1,1024]{1,0:T(1,128)} %param.17) | copy-start | bytes 12292
  0.7 15.3 %copy-start.4 = (s32[1,128]{1,0:T(1,128)S(1)}, s32[1,128]{1,0:T(1,128)}, u32[]{:S(2)}) copy-start(s32[1,128]{1,0:T(1,128)} %param.18) | copy-start | bytes 1540
  0.7 15.3 %copy-start.5 = (s32[1,128,1]{1,2,0:T(1,128)S(1)}, s32[1,128,1]{1,2,0:T(1,128)}, u32[]{:S(2)}) copy-start(s32[1,128,1]{1,2,0:T(1,128)} %param.19) | copy-start | bytes 1540
  0.7 15.3 %copy-start.6 = (s32[1,128]{1,0:T(1,128)S(1)}, s32[1,128]{1,0:T(1,128)}, u32[]{:S(2)}) copy-start(s32[1,128]{1,0:T(1,128)} %tile_ref.1) | copy-start | bytes 1540
  3.2 12.6 %collective-permute-start.2 = (f32[4,512]{1,0:T(4,128)}, f32[4,512]{1,0:T(4,128)S(1)}, u32[]{:S(2)}, u32[]{:S(2)}) collective-permute-start(f32[4,512]{1,0:T(4,128)} %get-tuple-element.14), channel_id=1, source_target_pairs={{0,1},{1,0},{2,3},{3,2},{4,5},{5,4},{6,7},{7,6},{8,9},{9,8},{10,11... | collective-permute-start | bytes 24584 | tf_op jit(solution)/shard_map/ppermute | solution.py:452
  5.4 10.6 %collective-permute-start.3 = (f32[4,512]{1,0:T(4,128)}, f32[4,512]{1,0:T(4,128)S(1)}, u32[]{:S(2)}, u32[]{:S(2)}) collective-permute-start(f32[4,512]{1,0:T(4,128)} %get-tuple-element.15), channel_id=1, source_target_pairs={{0,127},{1,2},{2,1},{3,4},{4,3},{5,6},{6,5},{7,8},{8,7},{9,10},{10... | collective-permute-start | bytes 24584 | tf_op jit(solution)/shard_map/ppermute | solution.py:453
  14.8 17.5 %collective-permute-start = (f32[4,80,512]{2,1,0:T(8,128)}, f32[4,80,512]{2,1,0:T(8,128)S(1)}, u32[]{:S(2)}, u32[]{:S(2)}) collective-permute-start(f32[4,80,512]{2,1,0:T(8,128)} %get-tuple-element.12), channel_id=1, source_target_pairs={{0,1},{1,0},{2,3},{3,2},{4,5},{5,4},{6,7},{7,6},{8,9},{9,8},{10,11... | collective-permute-start | bytes 1966088 | tf_op jit(solution)/shard_map/ppermute | solution.py:454
  14.8 20.6 %collective-permute-start.1 = (f32[4,80,512]{2,1,0:T(8,128)}, f32[4,80,512]{2,1,0:T(8,128)S(1)}, u32[]{:S(2)}, u32[]{:S(2)}) collective-permute-start(f32[4,80,512]{2,1,0:T(8,128)} %get-tuple-element.13), channel_id=1, source_target_pairs={{0,127},{1,2},{2,1},{3,4},{4,3},{5,6},{6,5},{7,8},{8,7},{9,10},{10... | collective-permute-start | bytes 1966088 | tf_op jit(solution)/shard_map/ppermute | solution.py:455
  16.1 20.2 %copy-start = (s32[1,16]{1,0:T(1,128)S(1)}, s32[1,16]{1,0:T(1,128)}, u32[]{:S(2)}) copy-start(s32[1,16]{1,0:T(1,128)} %param.14) | copy-start | bytes 196
  21.2 29.0 %all-to-all-start = ((f32[128,1,1152]{2,1,0:T(1,128)}), f32[128,1,1152]{2,1,0:T(1,128)}, u32[]{:S(2)}, u32[]{:S(2)}) async-start(f32[128,1,1152]{2,1,0:T(1,128)} %bitcast.9), calls=%async_computation | async-start | bytes 1179648 | tf_op jit(solution)/shard_map/all_to_all | solution.py:460
  32.3 3.1 %copy-start.8 = (f32[4,80,512]{2,1,0:T(8,128)}, f32[4,80,512]{2,1,0:T(8,128)S(1)}, u32[]{:S(2)}) copy-start(f32[4,80,512]{2,1,0:T(8,128)S(1)} %collective-permute-done.one_ref) | copy-start | bytes 1966084
  35.4 0.9 %copy-start.9 = (f32[4,80,512]{2,1,0:T(8,128)}, f32[4,80,512]{2,1,0:T(8,128)S(1)}, u32[]{:S(2)}) copy-start(f32[4,80,512]{2,1,0:T(8,128)S(1)} %collective-permute-done.1.two_ref) | copy-start | bytes 1966084
  50.2 6.5 %collective-permute-start.4 = (f32[128,1,1152]{2,1,0:T(1,128)}, f32[128,1,1152]{2,1,0:T(1,128)S(1)}, u32[]{:S(2)}, u32[]{:S(2)}) collective-permute-start(f32[128,1,1152]{2,1,0:T(1,128)} %shard_map.125), channel_id=1, source_target_pairs={{0,128},{128,0},{1,129},{129,1},{2,130},{130,2},{3,131},{131,3},{4... | collective-permute-start | bytes 1769480 | tf_op jit(solution)/shard_map/ppermute | solution.py:466

commit v3 on v2

--- a/solution.py
+++ b/solution.py
@@ -148,7 +148,9 @@
     for tile in range(tiles):
         where = slice(tile * LANES, (tile + 1) * LANES)
         here = window[:, 0, where]
-        mixed = jnp.dot(here, ops_ref[tile], precision=lax.Precision.HIGHEST, preferred_element_type=F32)
+        both = jnp.concatenate(split2(ops_ref[tile]), axis=1)
+        mixed = mm(jnp.concatenate(split2(here), axis=1), jnp.concatenate([both, both], axis=0))
+        mixed = mixed[:, :LANES] + mixed[:, LANES:]
         base = tile * (fields + 1)
         total = spread[base + fields : base + fields + 1]
         total_ref[:, where] = jnp.broadcast_to(total, (total_ref.shape[0], LANES))

time: 60.3 us -> 59.8 us (level)
  transfers between devices with their start and end apart: 6 -> 6, of which waited for: 4 -> 4; matrix products, arithmetic and copies ran while one was open for 0% -> 0% of each run, Pallas kernels for 31% -> 30%
where the time goes in v3:
time: 59.8 us; the launch traced here: 59.6 us
  starting transfers between devices  28.3 us (47%)
  Pallas kernels  23.7 us (40%)
  waiting for transfers between devices  5.88 us (10%)
  local copies, waits for them, and re-layouts  0.89 us (1%)
  between operations  0.79 us (1%)
    pallas_call x1, Pallas kernels, column_part(): pl.pallas_call(column_body, grid=(steps,), in_specs=[whole(x) for x in (o...  13.3 us
    all_to_all x1, starting transfers between devices, local(): lax.all_to_all(outgoing.reshape(group, 1, CHUNK * LANES), axes, split_axi...  11 us
    ppermute x1, starting transfers between devices, local(): top_two = lax.ppermute(top_two, axes, second)  9.39 us
    ppermute x1, starting transfers between devices, local(): arrived = lax.ppermute(after(arrived, token), 'comp', [(0, 1), (1, 0)])  4.68 us
    pallas_call x1, Pallas kernels, remap(): pl.pallas_call(remap_body, in_specs=[vspec()] * 2 + [aspec()] + [vspec()]...  4.67 us
    ppermute x1, waiting for transfers between devices, local(): two = lax.ppermute(two, axes, second)  3.61 us
    pallas_call x1, Pallas kernels, finish(): pl.pallas_call(finish_body, in_specs=[vspec(), vspec(), vspec(), sspec()]...  3.29 us
    pallas_call x1, Pallas kernels, pack(): pl.pallas_call(pack_body, in_specs=[sspec(), aspec()], out_specs=[vspec()...  2.45 us
  transfers between devices with their start and end apart: 6, of which 4 were waited for; matrix products, arithmetic and copies ran while one was open for 0% of the time, Pallas kernels for 30%

profile of v3, /device:TPU:1, one launch (start us, length us, event | category | flops | bytes accessed | tf_op | source)
XLA Modules:
  0.0 59.6 jit_solution(10114863413371022878)
XLA Ops:
  0.6 0.0 copy-start.7
  0.7 0.0 copy-start.1
  0.7 0.0 copy-start.2
  0.7 0.0 copy-start.3
  0.7 0.0 copy-start.4
  0.7 0.0 copy-start.5
  0.7 0.0 copy-start.6
  0.7 2.4 %shard_map.122 = (f32[4,512]{1,0:T(4,128)}, f32[4,512]{1,0:T(4,128)}, f32[4,80,512]{2,1,0:T(8,128)}, f32[4,80,512]{2,1,0:T(8,128)}) custom-call(s32[1]{0:T(128)} %bitcast.even_ref, f32[1,4,80,2048]{3,2,1,0:T(8,128)} %state_ref.5), custom_call_target="tpu_custom_call" | custom-call | flops 60000002048 | bytes 3000000 | tf_op jit(solution)/shard_map/pallas_call | solution.py:77
  3.2 2.2 %collective-permute-start.2 = (f32[4,512]{1,0:T(4,128)}, f32[4,512]{1,0:T(4,128)S(1)}, u32[]{:S(2)}, u32[]{:S(2)}) collective-permute-start(f32[4,512]{1,0:T(4,128)} %get-tuple-element.14), channel_id=1, source_target_pairs={{0,1},{1,0},{2,3},{3,2},{4,5},{5,4},{6,7},{7,6},{8,9},{9,8},{10,11... | collective-permute-start | bytes 24584 | tf_op jit(solution)/shard_map/ppermute | solution.py:454
  5.4 9.4 %collective-permute-start.3 = (f32[4,512]{1,0:T(4,128)}, f32[4,512]{1,0:T(4,128)S(1)}, u32[]{:S(2)}, u32[]{:S(2)}) collective-permute-start(f32[4,512]{1,0:T(4,128)} %get-tuple-element.15), channel_id=1, source_target_pairs={{0,127},{1,2},{2,1},{3,4},{4,3},{5,6},{6,5},{7,8},{8,7},{9,10},{10... | collective-permute-start | bytes 24584 | tf_op jit(solution)/shard_map/ppermute | solution.py:455
  14.8 0.0 collective-permute-start
  14.8 1.0 %collective-permute-start.1 = (f32[4,80,512]{2,1,0:T(8,128)}, f32[4,80,512]{2,1,0:T(8,128)S(1)}, u32[]{:S(2)}, u32[]{:S(2)}) collective-permute-start(f32[4,80,512]{2,1,0:T(8,128)} %get-tuple-element.13), channel_id=1, source_target_pairs={{0,127},{1,2},{2,1},{3,4},{4,3},{5,6},{6,5},{7,8},{8,7},{9,10},{10... | collective-permute-start | bytes 1966088 | tf_op jit(solution)/shard_map/ppermute | solution.py:457
  15.8 0.0 copy-done.7
  15.8 0.0 collective-permute-done.2.one_ref
  15.8 0.2 collective-permute-done.3.two_ref
  16.0 0.0 copy-done.1
  16.0 0.0 copy-done.3
  16.0 0.0 copy-done.4
  16.0 0.0 copy-done.5
  16.1 0.0 copy-done.6
  16.1 0.0 copy-start
  16.1 4.7 %shard_map.123 = (f32[4,2048]{1,0:T(4,128)S(1)}, f32[8,2048]{1,0:T(8,128)S(1)}, f32[1152,128]{1,0:T(8,128)}) custom-call(f32[4,512]{1,0:T(4,128)S(1)} %collective-permute-done.2.one_ref, f32[4,512]{1,0:T(4,128)S(1)} %collective-permute-done.3.two_ref, f32[1,4,80,2048]{3,2,1,0:T(8,128)} %state_ref.5, f32[16,128,128]{2,1,0:T(8,128)S(1)} %bitcast.17, ...), custom_call_target="tpu_custom_call" | custom-call | flops 60000002048 | bytes 6000000 | tf_op jit(solution)/shard_map/pallas_call | solution.py:202
  20.8 11.0 %all-to-all-start = ((f32[128,1,1152]{2,1,0:T(1,128)}), f32[128,1,1152]{2,1,0:T(1,128)}, u32[]{:S(2)}, u32[]{:S(2)}) async-start(f32[128,1,1152]{2,1,0:T(1,128)} %bitcast.9), calls=%async_computation | async-start | bytes 1179648 | tf_op jit(solution)/shard_map/all_to_all | solution.py:462
  31.8 0.0 collective-permute-done.one_ref
  31.8 0.0 copy-start.8
  31.8 3.6 %collective-permute-done.1.two_ref = f32[4,80,512]{2,1,0:T(8,128)S(1)} collective-permute-done((f32[4,80,512]{2,1,0:T(8,128)}, f32[4,80,512]{2,1,0:T(8,128)S(1)}, u32[]{:S(2)}, u32[]{:S(2)}) %collective-permute-start.1) | collective-permute-done | bytes 655392 | tf_op jit(solution)/shard_map/ppermute | solution.py:457
  35.4 0.8 %copy-done.9 = f32[4,80,512]{2,1,0:T(8,128)} copy-done((f32[4,80,512]{2,1,0:T(8,128)}, f32[4,80,512]{2,1,0:T(8,128)S(1)}, u32[]{:S(2)}) %copy-start.9) | copy-done | bytes 655384
  36.3 13.3 %shard_map.124 = (f32[4,80,2048]{2,1,0:T(8,128)S(1)}, f32[80,2048]{1,0:T(8,128)S(1)}, f32[8,128]{1,0:T(8,128)}) custom-call(f32[4,80,512]{2,1,0:T(8,128)} %copy-done.8, f32[4,80,512]{2,1,0:T(8,128)} %copy-done.9, s32[8,128]{1,0:T(8,128)S(1)} %bitcast.19, s32[8,128]{1,0:T(8,128)S(1)} %bitcast.13, f32[8,128]{1,0:T(8,128)S(1)} %bitcast.21, ...), custom_call_target="tpu_custom_call" | custom-call | flops 60000002048 | bytes 10000000 | tf_op jit(solution)/shard_map/pallas_call | solution.py:330
  49.6 0.2 all-to-all-done.value_ref
  49.8 4.7 %collective-permute-start.4 = (f32[128,1,1152]{2,1,0:T(1,128)}, f32[128,1,1152]{2,1,0:T(1,128)S(1)}, u32[]{:S(2)}, u32[]{:S(2)}) collective-permute-start(f32[128,1,1152]{2,1,0:T(1,128)} %shard_map.125), channel_id=1, source_target_pairs={{0,128},{128,0},{1,129},{129,1},{2,130},{130,2},{3,131},{131,3},{4... | collective-permute-start | bytes 1769480 | tf_op jit(solution)/shard_map/ppermute | solution.py:468
  54.4 1.8 %collective-permute-done.4 = f32[128,1,1152]{2,1,0:T(1,128)S(1)} collective-permute-done((f32[128,1,1152]{2,1,0:T(1,128)}, f32[128,1,1152]{2,1,0:T(1,128)S(1)}, u32[]{:S(2)}, u32[]{:S(2)}) %collective-permute-start.4) | collective-permute-done | bytes 589856 | tf_op jit(solution)/shard_map/ppermute | solution.py:468
  56.3 3.3 %shard_map.126 = (f32[1,4,80,2048]{3,2,1,0:T(8,128)}, f32[1,4,2048]{2,1,0:T(4,128)}) custom-call(f32[4,80,2048]{2,1,0:T(8,128)S(1)} %get-tuple-element.18.base_ref, f32[80,2048]{1,0:T(8,128)S(1)} %get-tuple-element.19.gain_ref, f32[1152,128]{1,0:T(8,128)S(1)} %bitcast.11, s32[16]{0:T(128)S(1)} %bitcast.15), custom_call_target="tpu_custom_call" | custom-call | flops 10000000 | bytes 6000000 | tf_op jit(solution)/shard_map/pallas_call | solution.py:405
  (6 shorter events, 0.0 us)
Async XLA Ops:
  0.6 15.1 %copy-start.7 = (s32[1,1024]{1,0:T(1,128)S(1)}, s32[1,1024]{1,0:T(1,128)}, u32[]{:S(2)}) copy-start(s32[1,1024]{1,0:T(1,128)} %param.16) | copy-start | bytes 12292
  0.7 15.4 %copy-start.1 = (f32[1,16,128,128]{3,2,1,0:T(8,128)S(1)}, f32[1,16,128,128]{3,2,1,0:T(8,128)}, u32[]{:S(2)}) copy-start(f32[1,16,128,128]{3,2,1,0:T(8,128)} %param.12) | copy-start | bytes 3145732
  0.7 15.4 %copy-start.2 = (s32[1,1024]{1,0:T(1,128)S(1)}, s32[1,1024]{1,0:T(1,128)}, u32[]{:S(2)}) copy-start(s32[1,1024]{1,0:T(1,128)} %param.15) | copy-start | bytes 12292
  0.7 15.4 %copy-start.3 = (f32[1,1024]{1,0:T(1,128)S(1)}, f32[1,1024]{1,0:T(1,128)}, u32[]{:S(2)}) copy-start(f32[1,1024]{1,0:T(1,128)} %param.17) | copy-start | bytes 12292
  0.7 15.3 %copy-start.4 = (s32[1,128]{1,0:T(1,128)S(1)}, s32[1,128]{1,0:T(1,128)}, u32[]{:S(2)}) copy-start(s32[1,128]{1,0:T(1,128)} %param.18) | copy-start | bytes 1540
  0.7 15.3 %copy-start.5 = (s32[1,128,1]{1,2,0:T(1,128)S(1)}, s32[1,128,1]{1,2,0:T(1,128)}, u32[]{:S(2)}) copy-start(s32[1,128,1]{1,2,0:T(1,128)} %param.19) | copy-start | bytes 1540
  0.7 15.3 %copy-start.6 = (s32[1,128]{1,0:T(1,128)S(1)}, s32[1,128]{1,0:T(1,128)}, u32[]{:S(2)}) copy-start(s32[1,128]{1,0:T(1,128)} %tile_ref.1) | copy-start | bytes 1540
  3.2 12.6 %collective-permute-start.2 = (f32[4,512]{1,0:T(4,128)}, f32[4,512]{1,0:T(4,128)S(1)}, u32[]{:S(2)}, u32[]{:S(2)}) collective-permute-start(f32[4,512]{1,0:T(4,128)} %get-tuple-element.14), channel_id=1, source_target_pairs={{0,1},{1,0},{2,3},{3,2},{4,5},{5,4},{6,7},{7,6},{8,9},{9,8},{10,11... | collective-permute-start | bytes 24584 | tf_op jit(solution)/shard_map/ppermute | solution.py:454
  5.4 10.6 %collective-permute-start.3 = (f32[4,512]{1,0:T(4,128)}, f32[4,512]{1,0:T(4,128)S(1)}, u32[]{:S(2)}, u32[]{:S(2)}) collective-permute-start(f32[4,512]{1,0:T(4,128)} %get-tuple-element.15), channel_id=1, source_target_pairs={{0,127},{1,2},{2,1},{3,4},{4,3},{5,6},{6,5},{7,8},{8,7},{9,10},{10... | collective-permute-start | bytes 24584 | tf_op jit(solution)/shard_map/ppermute | solution.py:455
  14.8 17.0 %collective-permute-start = (f32[4,80,512]{2,1,0:T(8,128)}, f32[4,80,512]{2,1,0:T(8,128)S(1)}, u32[]{:S(2)}, u32[]{:S(2)}) collective-permute-start(f32[4,80,512]{2,1,0:T(8,128)} %get-tuple-element.12), channel_id=1, source_target_pairs={{0,1},{1,0},{2,3},{3,2},{4,5},{5,4},{6,7},{7,6},{8,9},{9,8},{10,11... | collective-permute-start | bytes 1966088 | tf_op jit(solution)/shard_map/ppermute | solution.py:456
  14.8 20.6 %collective-permute-start.1 = (f32[4,80,512]{2,1,0:T(8,128)}, f32[4,80,512]{2,1,0:T(8,128)S(1)}, u32[]{:S(2)}, u32[]{:S(2)}) collective-permute-start(f32[4,80,512]{2,1,0:T(8,128)} %get-tuple-element.13), channel_id=1, source_target_pairs={{0,127},{1,2},{2,1},{3,4},{4,3},{5,6},{6,5},{7,8},{8,7},{9,10},{10... | collective-permute-start | bytes 1966088 | tf_op jit(solution)/shard_map/ppermute | solution.py:457
  16.1 20.2 %copy-start = (s32[1,16]{1,0:T(1,128)S(1)}, s32[1,16]{1,0:T(1,128)}, u32[]{:S(2)}) copy-start(s32[1,16]{1,0:T(1,128)} %param.14) | copy-start | bytes 196
  20.8 29.0 %all-to-all-start = ((f32[128,1,1152]{2,1,0:T(1,128)}), f32[128,1,1152]{2,1,0:T(1,128)}, u32[]{:S(2)}, u32[]{:S(2)}) async-start(f32[128,1,1152]{2,1,0:T(1,128)} %bitcast.9), calls=%async_computation | async-start | bytes 1179648 | tf_op jit(solution)/shard_map/all_to_all | solution.py:462
  31.8 3.6 %copy-start.8 = (f32[4,80,512]{2,1,0:T(8,128)}, f32[4,80,512]{2,1,0:T(8,128)S(1)}, u32[]{:S(2)}) copy-start(f32[4,80,512]{2,1,0:T(8,128)S(1)} %collective-permute-done.one_ref) | copy-start | bytes 1966084
  35.4 0.9 %copy-start.9 = (f32[4,80,512]{2,1,0:T(8,128)}, f32[4,80,512]{2,1,0:T(8,128)S(1)}, u32[]{:S(2)}) copy-start(f32[4,80,512]{2,1,0:T(8,128)S(1)} %collective-permute-done.1.two_ref) | copy-start | bytes 1966084
  49.8 6.5 %collective-permute-start.4 = (f32[128,1,1152]{2,1,0:T(1,128)}, f32[128,1,1152]{2,1,0:T(1,128)S(1)}, u32[]{:S(2)}, u32[]{:S(2)}) collective-permute-start(f32[128,1,1152]{2,1,0:T(1,128)} %shard_map.125), channel_id=1, source_target_pairs={{0,128},{128,0},{1,129},{129,1},{2,130},{130,2},{3,131},{131,3},{4... | collective-permute-start | bytes 1769480 | tf_op jit(solution)/shard_map/ppermute | solution.py:468
